TPU v7x, 256 devices: a whole 4x4x8 slice. The times are simulated.
256 devices in a mesh: row: 8 (over z), col: 16 (over y, x), aux: 2 (over core).
Axes of the slice: x: 4, y: 4, z: 8, core: 2. Of those that a mesh axis runs over, the one named last changes fastest.
Arguments:
- panels: bfloat16 [64, 43200], P(('aux', 'row'), 'col'), may hold values from -6 to 6
- amplitudes: bfloat16 [10800, 43200], P('row', 'col'), may hold values from -0.03125 to 0.03125
- virt_coeff: bfloat16 [1500, 1350], replicated, may hold values from -0.15625 to 0.15625
- row_owner: int32 [1500, 1], replicated, may hold values from 0 to 127; in each aligned block of 1500 rows (0 to 1499, 1500 to 2999, ...) at most 24 rows name the same one
Outputs:
- delivered: bfloat16 [3072, 512], P(('row', 'col'), 'aux')
Inputs may be any that keep to these rules, and one draw needn't show every extreme that they name: `row_owner`: no owner is named by more than 24 AO functions, a bound that some block reaches.
All inputs are finite; a program needn't handle non-finite values.
Results may differ from a plain program's by a relative error of at most 0.0017.
Values may be sent and summed in bfloat16 or wider, within the bound.
A program may use at most 64 MiB of HBM per device.

v0:
```python
import jax
import jax.numpy as jnp
from jax import lax
from jax.sharding import PartitionSpec as P


def owner_slots(row_owner, count, capacity):
    owners = row_owner[:, 0]
    onehot = (owners[:, None] == jnp.arange(count, dtype=jnp.int32)[None, :]).astype(jnp.int32)
    running = jnp.cumsum(onehot, axis=0) - 1
    slot = jnp.sum(running * onehot, axis=1)
    return owners * capacity + slot


def shards(panels, amplitudes, virt_coeff, row_owner):
    rows_n = lax.axis_size("row")
    cols_n = lax.axis_size("col")
    count = rows_n * cols_n
    nao = virt_coeff.shape[0]
    virt = virt_coeff.shape[1]
    capacity = 2 * ((nao + count - 1) // count)
    occ_dev = amplitudes.shape[0] // virt
    target = owner_slots(row_owner, count, capacity)
    partial_value = lax.dot_general(
        lax.all_gather(panels, "row", axis=0, tiled=True),
        amplitudes,
        (((1,), (1,)), ((), ())),
        preferred_element_type=jnp.float32,
    )
    gamma = lax.psum_scatter(partial_value, "col", scatter_dimension=0, tiled=True)
    local_q = gamma.shape[0]
    half = jnp.dot(gamma, virt_coeff.T, precision=lax.Precision.HIGHEST)
    half = half.astype(jnp.bfloat16)
    outgoing = jnp.zeros((count * capacity, local_q * occ_dev), jnp.bfloat16).at[target].set(half.T)
    arrived = lax.all_to_all(
        outgoing.reshape(count, capacity * local_q * occ_dev),
        ("row", "col"),
        split_axis=0,
        concat_axis=0,
        tiled=True,
    )
    arrived = arrived.reshape(rows_n, cols_n, capacity, local_q, occ_dev)
    arrived = jnp.transpose(arrived, (2, 1, 3, 0, 4))
    return arrived.reshape(capacity, cols_n * local_q * rows_n * occ_dev)


def solution(mesh):
    placed = (P(("aux", "row"), "col"), P("row", "col"), P(), P())
    return jax.shard_map(
        shards, mesh=mesh, in_specs=placed, out_specs=P(("row", "col"), "aux"), check_vma=False
    )
```

profile of v0, /device:TPU:8, one launch (start us, length us, event | category | flops | bytes accessed | tf_op | source)
XLA Modules:
  0.0 176.1 jit_solution(17215622181932020998)
XLA Ops:
  6.5 0.0 copy-start
  6.5 0.0 all-reduce.4.cloned.1.call-start
  6.5 28.7 %all-gather = bf16[8,4,2700]{2,1,0:T(4,128)(2,1)S(1)} all-gather(bf16[1,4,2700]{2,1,0:T(4,128)(2,1)} %bitcast.23), channel_id=1, replica_groups=mesh['row'=8,'col'=16,'aux'=2] {'row'}, dimensions={0}, use_global_device_ids=true | all-gather | bytes 194400 | tf_op jit(solution)/shard_map/all_gather | solution.py:25
  35.3 0.1 reshape.37
  35.3 0.0 copy-start.1
  35.3 6.1 %fusion.10 = f32[32,1350]{1,0:T(8,128)} fusion(bf16[32,2700]{1,0:T(8,128)(2,1)S(1)} %reshape.37, bf16[1350,2700]{1,0:T(8,128)(2,1)} %param.5), kind=kOutput, calls=%fused_computation.19 | convolution fusion | flops 233280000 | bytes 7635600 | tf_op jit(solution)/shard_map/dot_general | solution.py:24
  41.4 0.0 all-reduce.4.cloned.1.call-update
  41.4 0.0 copy-done
  41.5 0.3 iota_compare_fusion
  41.8 0.1 pad_convert_fusion
  41.8 0.5 fusion.1
  42.3 0.1 broadcast_add_fusion
  42.4 0.3 copy.14
  42.7 0.5 fusion.4
  43.2 0.0 copy-done.1
  43.2 0.6 dynamic-slice
  44.5 88.9 %all-reduce.4.cloned.1.call-done = f32[32,1350]{1,0:T(8,128)} async-done(((f32[32,1350]{1,0:T(8,128)}), f32[32,1350]{1,0:T(8,128)}) %all-reduce.4.cloned.1.call-update) | async-done | bytes 172816
  133.3 3.9 %fusion = bf16[1500,2]{0,1:T(2,128)(2,1)S(1)} fusion(bf16[1500,1350]{0,1:T(8,128)(2,1)} %param.6, f32[32,1350]{1,0:T(8,128)} %all-reduce.4.cloned.1.call-done, u32[]{:T(128)S(6)} %multiply.1), kind=kOutput, calls=%fused_computation.2 | convolution fusion | flops 48603000 | bytes 4170612 | tf_op jit(solution)/shard_map/dot_general | solution.py:32
  137.3 0.3 copy.15
  137.6 6.6 %scatter_custom_fusion = bf16[3072,2]{1,0:T(8,128)(2,1)S(1)} fusion(s32[1500]{0:T(1024)S(1)} %fusion.8, bf16[1500,2]{1,0:T(8,128)(2,1)S(1)} %copy.15, bf16[]{:T(256)} %constant.6.clone.1), kind=kCustom, calls=%fused_computation.12 | custom fusion | bytes 12290 | tf_op jit(solution)/shard_map/scatter | solution.py:34
  144.2 0.5 all_to_all.8
  144.7 23.5 %all_to_all.10 = bf16[128,1,48]{2,1,0:T(2,128)(2,1)S(1)} all-to-all(bf16[128,1,48]{2,1,0:T(2,128)(2,1)S(1)} %all_to_all.8), channel_id=1, replica_groups=mesh['row'=8,'col'=16,'aux'=2] {'row','col'}, dimensions={0} | all-to-all | bytes 24576 | tf_op jit(solution)/shard_map/all_to_all | solution.py:35
  168.2 0.1 copy.17
  168.2 0.1 reshape.25
  168.4 0.2 copy.18
  168.5 0.7 copy.19
  (4 shorter events, 0.1 us)
Async XLA Ops:
  6.5 34.9 %copy-start = (s32[1500,1]{0,1:T(1,128)S(1)}, s32[1500,1]{0,1:T(1,128)}, u32[]{:S(2)}) copy-start(s32[1500,1]{0,1:T(1,128)} %param.7) | copy-start | bytes 18004
  6.5 126.8 %all-reduce.4.cloned.1.call-start = ((), (), s32[]{:S(2)}) async-start(), calls=%async_computation.1 | async-start | bytes 360448
  35.3 7.8 %copy-start.1 = (u32[256]{0:T(256)S(1)}, u32[256]{0:T(256)}, u32[]{:S(2)}) copy-start(u32[256]{0:T(256)} %constant.24) | copy-start | bytes 3076
Sparse Core Ops, SparseCore 0:
  41.6 91.7 all-reduce.3
where the time goes:
time: 176 us
  waiting for transfers between devices  88.9 us (51%)
  blocking collectives  52.2 us (30%)
  between operations  14.2 us (8%)
  matrix products  10 us (6%)
  local copies, waits for them, and re-layouts  9.38 us (5%)
    unnamed x2, waiting for transfers between devices  88.9 us
    all_gather x1, blocking collectives, shards(): lax.all_gather(panels, 'row', axis=0, tiled=True)  28.7 us
    all_to_all x1, blocking collectives, shards(): lax.all_to_all(outgoing.reshape(count, capacity * local_q * occ_dev), ('r...  23.5 us
    scatter x1, local copies, waits for them, and re-layouts, shards(): jnp.zeros((count * capacity, local_q * occ_dev), jnp.bfloat16).at[target]  6.65 us
    dot_general x1, matrix products, shards(): lax.dot_general(lax.all_gather(panels, 'row', axis=0, tiled=True), amplit...  6.08 us
    dot_general x1, matrix products, shards(): half = jnp.dot(gamma, virt_coeff.T, precision=lax.Precision.HIGHEST)  3.92 us
  transfers between devices with their start and end apart: 1, of which 1 were waited for; matrix products, arithmetic and copies ran while one was open for 1% of the time, Pallas kernels for 0%

commit v1 on v0

v1 whole, which is shorter than its diff:
```python
import functools
import jax
import jax.numpy as jnp
from jax import lax
from jax.experimental import pallas as pl
from jax.experimental.pallas import tpu as pltpu
from jax.sharding import PartitionSpec as P

F32 = jnp.float32
BF16 = jnp.bfloat16
MESH = pl.DeviceIdType.MESH
NT = (((1,), (1,)), ((), ()))

LANES = 128
GROUPS = 4
CHUNK = 24
SIX = 6
EIGHT = 8


def split(x):
    hi = x.astype(BF16)
    lo = (x - hi.astype(F32)).astype(BF16)
    return hi, lo


def iota(shape, dim):
    return lax.broadcasted_iota(jnp.int32, shape, dim)


def kernel(
    rows_n,
    cols_n,
    panels,
    owner,
    amp,
    coeff_t,
    out,
    t_buf,
    w_buf,
    x_stage,
    x_all,
    g_t,
    own_pad,
    code,
    sel,
    expand,
    d_buf,
    r_buf,
    s_all,
    z_buf,
    z_all,
    o_buf,
    local_sem,
    xs,
    xr,
    ds,
    dr,
    ss,
    sr,
    zs,
    zr,
):
    me_r = lax.axis_index("row")
    me_c = lax.axis_index("col")
    q_own, depth = panels.shape
    virt, nao = coeff_t.shape
    q_dev = rows_n * q_own
    block = x_stage.shape[1]
    stride = CHUNK * cols_n

    cp_w = pltpu.make_async_copy(coeff_t, w_buf, local_sem.at[0])
    cp_t = pltpu.make_async_copy(amp, t_buf, local_sem.at[1])
    cp_w.start()
    cp_t.start()

    barrier = pltpu.get_barrier_semaphore()

    @pl.loop(1, rows_n)
    def _(k):
        pl.semaphore_signal(
            barrier, inc=1, device_id={"row": lax.rem(me_r + k, rows_n)}, device_id_type=MESH
        )

    @pl.loop(1, cols_n)
    def _(k):
        pl.semaphore_signal(
            barrier, inc=1, device_id={"col": lax.rem(me_c + k, cols_n)}, device_id_type=MESH
        )

    x_stage[...] = jnp.zeros_like(x_stage)
    for kb in range(GROUPS):
        width = min(block, depth - kb * block)
        x_stage[pl.ds(kb * q_own, q_own), pl.ds(0, width)] = panels[
            :, pl.ds(kb * block, width)
        ].astype(F32)
    tall = GROUPS * q_own
    x_all[pl.ds(pl.multiple_of(me_r * tall, tall), tall), :] = x_stage[...].astype(BF16)

    pl.semaphore_wait(barrier, rows_n - 1 + cols_n - 1)

    def panel_copy(owner_r, to):
        rows = x_all.at[pl.ds(pl.multiple_of(owner_r * tall, tall), tall), :]
        return pltpu.make_async_remote_copy(
            src_ref=rows,
            dst_ref=rows,
            send_sem=xs.at[to],
            recv_sem=xr.at[owner_r],
            device_id={"row": to},
            device_id_type=MESH,
        )

    @pl.loop(1, rows_n)
    def _(k):
        panel_copy(me_r, lax.rem(me_r + k, rows_n)).start()

    own_pad[...] = jnp.full_like(own_pad, -1)
    own_pad[:, pl.ds(0, nao)] = owner[...]
    count = rows_n * cols_n
    tri = (iota((256, 256), 0) < iota((256, 256), 1)).astype(BF16)
    carry = jnp.zeros((count, 1), F32)
    for b in range(own_pad.shape[1] // 256):
        names = own_pad[:, pl.ds(b * 256, 256)]
        hot = names == iota((count, 256), 0)
        ones = jnp.where(hot, 1.0, 0.0).astype(F32)
        before = jnp.dot(ones.astype(BF16), tri, preferred_element_type=F32) + carry
        slot = jnp.sum(ones * before, axis=0, keepdims=True)
        carry = carry + jnp.sum(ones, axis=1, keepdims=True)
        group = (
            jnp.where(slot >= SIX, 1.0, 0.0)
            + jnp.where(slot >= 2 * SIX, 1.0, 0.0)
            + jnp.where(slot >= 3 * SIX, 1.0, 0.0)
        )
        at_row = lax.div(names, jnp.int32(cols_n))
        at_col = names - at_row * cols_n
        place = group * (rows_n * EIGHT - SIX) + slot + at_row.astype(F32) * EIGHT
        code[:, pl.ds(b * 256, 256)] = jnp.where(at_col == me_c, place, -1.0)
    wide = GROUPS * rows_n * EIGHT
    perm = jnp.where(code[:, pl.ds(0, nao)] == iota((wide, nao), 0).astype(F32), 1.0, 0.0).astype(BF16)
    sel[...] = jnp.zeros_like(sel)
    cp_w.wait()
    sel[:, pl.ds(0, virt)] = lax.dot_general(
        perm, w_buf[...], NT, preferred_element_type=F32
    ).astype(BF16)

    for i in range(rows_n):
        a = iota((LANES, q_dev * rows_n), 0)
        n = iota((LANES, q_dev * rows_n), 1)
        spread = jnp.where(lax.rem(a, q_dev) * rows_n + i == n, 1.0, 0.0)
        expand[pl.ds(i * LANES, LANES), :] = spread.astype(BF16)

    @pl.loop(1, rows_n)
    def _(k):
        panel_copy(lax.rem(me_r + k, rows_n), me_r).wait_recv()

    for kb in range(GROUPS):
        n = iota((LANES, LANES), 0)
        m = iota((LANES, LANES), 1)
        q = lax.rem(n, q_dev)
        source = lax.div(q, q_own) * tall + kb * q_own + lax.rem(q, q_own)
        pick = jnp.where(source == m, 1.0, 0.0).astype(BF16)
        g = jnp.dot(pick, x_all[...], preferred_element_type=F32)
        g_t[pl.ds(kb * block, block), :] = g.T.astype(BF16)

    def lane_group(shape):
        return lax.div(iota(shape, 1), q_dev)

    def partial_copy(source, to):
        return pltpu.make_async_remote_copy(
            src_ref=d_buf.at[pl.ds(pl.multiple_of(to * CHUNK, CHUNK), CHUNK), :],
            dst_ref=r_buf.at[pl.ds(pl.multiple_of(source * CHUNK, CHUNK), CHUNK), :],
            send_sem=ds.at[to],
            recv_sem=dr.at[source],
            device_id={"col": to},
            device_id_type=MESH,
        )

    cp_t.wait()
    steps = 4
    part = stride // steps
    for step in range(steps):
        pieces, sizes = [], []
        for g in range(GROUPS):
            start = g * stride + step * part
            size = max(0, min(part, virt - start))
            if size:
                pieces.append(t_buf[pl.ds(start, size), :])
            sizes.append(size)
        dense = jnp.zeros((part, LANES), F32)
        groups = lane_group((part, LANES))
        for g in range(GROUPS):
            if sizes[g]:
                value = jnp.dot(pieces[g], g_t[pl.ds(0, depth), :], preferred_element_type=F32)
                if sizes[g] < part:
                    d_buf[pl.ds(step * part, part), :] = jnp.zeros((part, LANES), F32)
                    d_buf[pl.ds(step * part, sizes[g]), :] = value
                    value = d_buf[pl.ds(step * part, part), :]
                dense = jnp.where(groups == g, value, dense)
        d_buf[pl.ds(step * part, part), :] = dense
        per = cols_n // steps
        for j in range(per):
            to = step * per + j

            @pl.when(to != me_c)
            def _():
                partial_copy(me_c, to).start()

    def mine(ref):
        return ref[pl.ds(pl.multiple_of(me_c * CHUNK, CHUNK), CHUNK), :]

    total = mine(d_buf)
    for k in range(1, cols_n):
        source = lax.rem(me_c + k, cols_n)
        partial_copy(source, me_c).wait_recv()
        total = total + r_buf[pl.ds(pl.multiple_of(source * CHUNK, CHUNK), CHUNK), :]
    s_all[pl.ds(pl.multiple_of(me_c * CHUNK, CHUNK), CHUNK), :] = total

    def sum_copy(source, to):
        rows = s_all.at[pl.ds(pl.multiple_of(source * CHUNK, CHUNK), CHUNK), :]
        return pltpu.make_async_remote_copy(
            src_ref=rows,
            dst_ref=rows,
            send_sem=ss.at[to],
            recv_sem=sr.at[source],
            device_id={"col": to},
            device_id_type=MESH,
        )

    @pl.loop(1, cols_n)
    def _(k):
        sum_copy(me_c, lax.rem(me_c + k, cols_n)).start()

    @pl.loop(1, cols_n)
    def _(k):
        sum_copy(lax.rem(me_c + k, cols_n), me_c).wait_recv()

    hi, lo = split(s_all[...])
    both = jnp.concatenate([hi, lo], axis=1)
    y = jnp.zeros((wide, LANES), F32)
    groups = lane_group((wide, LANES))
    for g in range(GROUPS):
        x = jnp.dot(sel[:, pl.ds(g * stride, stride)], both, preferred_element_type=F32)
        y = y + jnp.where(groups == g, x[:, :LANES] + x[:, LANES:], 0.0)
    y = y + pltpu.roll(y, 2 * q_dev, 1)
    y = y + pltpu.roll(y, q_dev, 1)
    tall_z = rows_n * EIGHT
    z = jnp.zeros((tall_z, LANES), F32)
    groups = lane_group((tall_z, LANES))
    for g in range(GROUPS):
        z = jnp.where(groups == g, y[g * tall_z : (g + 1) * tall_z, :], z)
    z_buf[...] = z

    def slot_copy(source, to):
        return pltpu.make_async_remote_copy(
            src_ref=z_buf.at[pl.ds(pl.multiple_of(to * EIGHT, EIGHT), EIGHT), :],
            dst_ref=z_all.at[pl.ds(pl.multiple_of(source * EIGHT, EIGHT), EIGHT), :],
            send_sem=zs.at[to],
            recv_sem=zr.at[source],
            device_id={"row": to},
            device_id_type=MESH,
        )

    @pl.loop(1, rows_n)
    def _(k):
        slot_copy(me_r, lax.rem(me_r + k, rows_n)).start()

    own_rows = pl.ds(pl.multiple_of(me_r * EIGHT, EIGHT), EIGHT)
    z_all[own_rows, :] = z_buf[own_rows, :]

    @pl.loop(1, rows_n)
    def _(k):
        slot_copy(lax.rem(me_r + k, rows_n), me_r).wait_recv()

    groups = lane_group((EIGHT, LANES))
    lefts = []
    for i in range(rows_n):
        got = z_all[pl.ds(i * EIGHT, EIGHT), :]
        left = [jnp.where(groups == g, got, 0.0) for g in range(GROUPS)]
        lefts.append(jnp.concatenate(left, axis=0))
    left = jnp.concatenate(lefts, axis=1).astype(BF16)
    result = jnp.dot(left, expand[...], preferred_element_type=F32)
    for g in range(GROUPS):
        o_buf[pl.ds(g * SIX, SIX), :] = result[g * EIGHT : g * EIGHT + SIX, :]
    out[...] = o_buf[...].astype(BF16)

    @pl.loop(1, rows_n)
    def _(k):
        to = lax.rem(me_r + k, rows_n)
        panel_copy(me_r, to).wait_send()
        slot_copy(me_r, to).wait_send()

    @pl.loop(1, cols_n)
    def _(k):
        to = lax.rem(me_c + k, cols_n)
        partial_copy(me_c, to).wait_send()
        sum_copy(me_c, to).wait_send()


def shards(panels, amplitudes, virt_coeff, row_owner):
    rows_n = lax.axis_size("row")
    cols_n = lax.axis_size("col")
    q_own, depth = panels.shape
    nao, virt = virt_coeff.shape
    q_dev = rows_n * q_own
    block = -(-depth // (GROUPS * LANES)) * LANES
    stride = CHUNK * cols_n
    wide = GROUPS * rows_n * EIGHT
    vmem = pltpu.VMEM
    dma = pltpu.SemaphoreType.DMA
    return pl.pallas_call(
        functools.partial(kernel, rows_n, cols_n),
        out_shape=jax.ShapeDtypeStruct((GROUPS * SIX, q_dev * rows_n), BF16),
        in_specs=[
            pl.BlockSpec(memory_space=pltpu.VMEM),
            pl.BlockSpec(memory_space=pltpu.VMEM),
            pl.BlockSpec(memory_space=pl.ANY),
            pl.BlockSpec(memory_space=pl.ANY),
        ],
        out_specs=pl.BlockSpec(memory_space=pltpu.VMEM),
        scratch_shapes=[
            vmem(amplitudes.shape, BF16),
            vmem((virt, nao), BF16),
            vmem((GROUPS * q_own, block), F32),
            vmem((LANES, block), BF16),
            vmem((GROUPS * block, LANES), BF16),
            vmem((1, -(-nao // 256) * 256), jnp.int32),
            vmem((1, -(-nao // 256) * 256), F32),
            vmem((wide, GROUPS * stride), BF16),
            vmem((rows_n * LANES, q_dev * rows_n), BF16),
            vmem((stride, LANES), F32),
            vmem((stride, LANES), F32),
            vmem((stride, LANES), F32),
            vmem((rows_n * EIGHT, LANES), F32),
            vmem((rows_n * EIGHT, LANES), F32),
            vmem((GROUPS * SIX, q_dev * rows_n), F32),
            dma((2,)),
            dma((rows_n,)),
            dma((rows_n,)),
            dma((cols_n,)),
            dma((cols_n,)),
            dma((cols_n,)),
            dma((cols_n,)),
            dma((rows_n,)),
            dma((rows_n,)),
        ],
        compiler_params=pltpu.CompilerParams(
            collective_id=0, has_side_effects=True, vmem_limit_bytes=56 * 1024 * 1024
        ),
        cost_estimate=pl.CostEstimate(
            flops=2 * virt * depth * LANES, bytes_accessed=amplitudes.size * 2, transcendentals=0
        ),
        name="density",
    )(panels, row_owner.reshape(1, nao), amplitudes, virt_coeff.T)


def solution(mesh):
    placed = (P(("aux", "row"), "col"), P("row", "col"), P(), P())
    return jax.shard_map(
        shards, mesh=mesh, in_specs=placed, out_specs=P(("row", "col"), "aux"), check_vma=False
    )
```

time: 176 us -> 37.3 us (0.21)
  waiting for transfers between devices: 88.9 us -> 0 us
  blocking collectives: 52.2 us -> 0 us
  Pallas kernels: 0 us -> 35.7 us
  between operations: 14.2 us -> 0.01 us
  matrix products: 10 us -> 0 us
  local copies, waits for them, and re-layouts: 9.38 us -> 1.31 us
    unnamed x2 -> x0, waiting for transfers between devices: 88.9 us -> none
    pallas_call x0 -> x1, Pallas kernels: none -> 35.7 us  [shards(): pl.pallas_call(functools.partial(kernel, rows_n, cols_n), out_shape=jax.S...]
    all_gather x1 -> x0, blocking collectives: 28.7 us -> none  [shards(): lax.all_gather(panels, 'row', axis=0, tiled=True)]
    all_to_all x1 -> x0, blocking collectives: 23.5 us -> none  [shards(): lax.all_to_all(outgoing.reshape(count, capacity * local_q * occ_dev), ('r...]
    dot_general x2 -> x0, matrix products: 10 us -> none  [the longest x1 6.08 us: shards(): lax.dot_general(lax.all_gather(panels, 'row', axis=0, tiled=True), amplit...]
    scatter x1 -> x0, local copies, waits for them, and re-layouts: 6.65 us -> none  [shards(): jnp.zeros((count * capacity, local_q * occ_dev), jnp.bfloat16).at[target]]
  transfers between devices with their start and end apart: 1 -> 0, of which waited for: 1 -> 0; matrix products, arithmetic and copies ran while one was open for 1% -> 0% of each run, Pallas kernels for 0% -> 0%
where the time goes in v1:
time: 37.3 us; the launch traced here: 37 us
  Pallas kernels  35.7 us (96%)
  local copies, waits for them, and re-layouts  1.31 us (4%)
    pallas_call x1, Pallas kernels, shards(): pl.pallas_call(functools.partial(kernel, rows_n, cols_n), out_shape=jax.S...  35.7 us
    unnamed x1, local copies, waits for them, and re-layouts  1.31 us

profile of v1, /device:TPU:8, one launch (start us, length us, event | category | flops | bytes accessed | tf_op | source)
XLA Modules:
  0.0 37.0 jit_solution(6017681907108846544)
XLA Ops:
  0.0 35.7 %density.1 = bf16[24,256]{1,0:T(8,128)(2,1)} custom-call(bf16[4,2700]{1,0:T(4,128)(2,1)} %panels.1, s32[1,1500]{1,0:T(1,128)} %bitcast.3, bf16[1350,2700]{1,0:T(8,128)(2,1)} %amp.1, bf16[1350,1500]{1,0:T(8,128)(2,1)} %bitcast.2), custom_call_target="tpu_custom_call" | custom-call | flops 933120000 | bytes 7290000 | tf_op jit(solution)/shard_map/density/pallas_call | solution.py:310
  35.7 1.3 %copy.6 = bf16[24,256]{1,0:T(8,128)(2,1)} copy(bf16[24,256]{1,0:T(8,128)(2,1)} %density.1) | data formatting | bytes 24576

commit v2 on v0

v2 whole, which is shorter than its diff:
```python
import functools
import jax
import jax.numpy as jnp
from jax import lax
from jax.experimental import pallas as pl
from jax.experimental.pallas import tpu as pltpu
from jax.sharding import PartitionSpec as P

F32 = jnp.float32
BF16 = jnp.bfloat16
MESH = pl.DeviceIdType.MESH
NT = (((1,), (1,)), ((), ()))

LANES = 128
BLOCKS = 4
WIDTH = 256
HEAD = 16
TAIL = 8
QUAD = 4


def split(x):
    hi = x.astype(BF16)
    lo = (x - hi.astype(F32)).astype(BF16)
    return jnp.concatenate([hi, lo], axis=0)


def iota(shape, dim):
    return lax.broadcasted_iota(jnp.int32, shape, dim)


def kernel(
    rows_n,
    cols_n,
    panels,
    owner,
    amp,
    coeff_t,
    out,
    t_buf,
    w_buf,
    p_buf,
    o_buf,
    names,
    x_stage,
    x_all,
    place,
    spread,
    expand,
    d_buf,
    r_buf,
    z_buf,
    z_all,
    local_sem,
    xs,
    xr,
    ds,
    dr,
    zs,
    zr,
):
    me_r = lax.axis_index("row")
    me_c = lax.axis_index("col")
    q_own, depth = panels.shape
    virt, nao = coeff_t.shape
    q_dev = rows_n * q_own
    chunks = x_all.shape[0]
    block = chunks * WIDTH
    tall = BLOCKS * q_own
    count = rows_n * cols_n
    dense = q_dev + q_dev // 2
    pair = 3 * LANES

    barrier = pltpu.get_barrier_semaphore()
    for k in range(1, rows_n):
        pl.semaphore_signal(
            barrier, inc=1, device_id={"row": lax.rem(me_r + k, rows_n)}, device_id_type=MESH
        )
    for k in range(1, cols_n):
        pl.semaphore_signal(
            barrier, inc=1, device_id={"col": lax.rem(me_c + k, cols_n)}, device_id_type=MESH
        )
    cp_p = pltpu.make_async_copy(panels, p_buf, local_sem.at[0])
    cp_o = pltpu.make_async_copy(owner, o_buf, local_sem.at[1])
    cp_t = pltpu.make_async_copy(amp, t_buf, local_sem.at[2])
    cp_w = pltpu.make_async_copy(coeff_t, w_buf, local_sem.at[3])
    cp_p.start()
    cp_o.start()
    cp_t.start()
    cp_w.start()

    x_stage[...] = jnp.zeros_like(x_stage)
    cp_p.wait()
    for kb in range(BLOCKS):
        width = min(block, depth - kb * block)
        x_stage[pl.ds(kb * q_own, q_own), pl.ds(0, width)] = p_buf[
            :, pl.ds(kb * block, width)
        ].astype(F32)
    own_rows = pl.ds(pl.multiple_of(me_r * tall, tall), tall)
    for t in range(chunks):
        x_all[t, own_rows, :] = x_stage[:, pl.ds(t * WIDTH, WIDTH)].astype(BF16)

    pl.semaphore_wait(barrier, rows_n - 1 + cols_n - 1)

    def panel_copy(t, source, to):
        rows = x_all.at[t, pl.ds(pl.multiple_of(source * tall, tall), tall), :]
        return pltpu.make_async_remote_copy(
            src_ref=rows,
            dst_ref=rows,
            send_sem=xs.at[t, to],
            recv_sem=xr.at[t, source],
            device_id={"row": to},
            device_id_type=MESH,
        )

    for t in range(chunks):
        for k in (4, 3, 5, 2, 6, 1, 7):
            panel_copy(t, me_r, lax.rem(me_r + k, rows_n)).start()

    names[...] = jnp.full_like(names, -1)
    cp_o.wait()
    names[:, pl.ds(0, nao)] = o_buf[...]
    tri = (iota((WIDTH, WIDTH), 0) < iota((WIDTH, WIDTH), 1)).astype(BF16)
    carry = jnp.zeros((count, 1), F32)
    for b in range(names.shape[1] // WIDTH):
        name = names[:, pl.ds(b * WIDTH, WIDTH)]
        ones = jnp.where(name == iota((count, WIDTH), 0), 1.0, 0.0).astype(F32)
        before = jnp.dot(ones.astype(BF16), tri, preferred_element_type=F32) + carry
        slot = jnp.sum(ones * before, axis=0, keepdims=True)
        carry = carry + jnp.sum(ones, axis=1, keepdims=True)
        at_row = lax.div(name, jnp.int32(cols_n))
        at_col = name - at_row * cols_n
        at_pair = lax.div(at_col, jnp.int32(2))
        odd = at_col - at_pair * 2
        base = (at_pair * pair + at_row * HEAD).astype(F32)
        early = base + (odd * LANES).astype(F32) + slot
        late = base + (odd * TAIL + (2 * LANES - HEAD)).astype(F32) + slot
        lane = jnp.where(slot < HEAD, early, late)
        lane = jnp.where(name < 0, -1.0, lane)
        place[pl.ds(b * WIDTH, WIDTH), :] = jnp.broadcast_to(lane, (LANES, WIDTH)).T

    @pl.loop(0, spread.shape[1] // LANES)
    def _(b):
        at = (iota((nao, LANES), 1) + b * LANES).astype(F32)
        hot = jnp.where(place[pl.ds(0, nao), :] == at, 1.0, 0.0)
        spread[:, pl.ds(pl.multiple_of(b * LANES, LANES), LANES)] = hot.astype(BF16)

    for i in range(rows_n):
        a = iota((LANES, rows_n * q_dev), 0)
        n = iota((LANES, rows_n * q_dev), 1)
        head = jnp.where((a < q_dev) & (n == a * rows_n + i), 1.0, 0.0)
        tail = jnp.where(
            (a >= q_dev) & (a < dense) & (lax.rem(n, LANES) == (a - q_dev) * rows_n + i), 1.0, 0.0
        )
        expand[pl.ds(i * LANES, LANES), :] = jnp.concatenate([head, tail], axis=1).astype(BF16)

    cp_t.wait()
    partial = jnp.zeros((q_dev, virt), F32)
    for t in range(chunks):

        @pl.loop(1, rows_n)
        def _(k):
            panel_copy(t, lax.rem(me_r + k, rows_n), me_r).wait_recv()

        for kb in range(BLOCKS):
            start = kb * block + t * WIDTH
            width = min(WIDTH, depth - start)
            if width <= 0:
                continue
            q = iota((q_dev, LANES), 0)
            source = lax.div(q, q_own) * tall + kb * q_own + lax.rem(q, q_own)
            pick = jnp.where(source == iota((q_dev, LANES), 1), 1.0, 0.0).astype(BF16)
            g = jnp.dot(pick, x_all[t], preferred_element_type=F32).astype(BF16)
            partial = partial + lax.dot_general(
                g[:, :width], t_buf[:, pl.ds(start, width)], NT, preferred_element_type=F32
            )

    cp_w.wait()
    half = jnp.dot(split(partial), w_buf[...], preferred_element_type=F32)
    half = split(half[:q_dev] + half[q_dev:])

    def partial_copy(source, to):
        return pltpu.make_async_remote_copy(
            src_ref=d_buf.at[to],
            dst_ref=r_buf.at[source],
            send_sem=ds.at[to],
            recv_sem=dr.at[source],
            device_id={"col": to},
            device_id_type=MESH,
        )

    quads = cols_n // QUAD
    my_quad = lax.div(me_c, QUAD)
    lower = lax.rem(iota((q_dev // 2, LANES), 1), 2 * TAIL) < TAIL
    for step in range(quads):
        quad = lax.rem(my_quad + (2, 1, 3, 0)[step], quads)
        lanes = QUAD // 2 * pair
        part = spread[:, pl.ds(pl.multiple_of(quad * lanes, lanes), lanes)]
        slots = jnp.dot(half, part, preferred_element_type=F32)
        slots = slots[:q_dev] + slots[q_dev:]
        for j in range(QUAD):
            to = quad * QUAD + j
            first = j // 2 * pair
            head = slots[:, first + j % 2 * LANES : first + (j % 2 + 1) * LANES]
            tail = slots[:, first + 2 * LANES : first + 3 * LANES]
            upper_q, lower_q = tail[: q_dev // 2], tail[q_dev // 2 :]
            if j % 2:
                upper_q = pltpu.roll(upper_q, LANES - TAIL, 1)
            else:
                lower_q = pltpu.roll(lower_q, TAIL, 1)
            d_buf[to, pl.ds(0, q_dev), :] = head
            d_buf[to, pl.ds(q_dev, q_dev // 2), :] = jnp.where(lower, upper_q, lower_q)

            @pl.when(to != me_c)
            def _():
                partial_copy(me_c, to).start()

    total = d_buf[me_c]
    for k in range(1, cols_n):
        source = lax.rem(me_c + k, cols_n)
        partial_copy(source, me_c).wait_recv()
        total = total + r_buf[source]
    total = jnp.concatenate([total, jnp.zeros((LANES - dense, LANES), F32)], axis=0)
    z_buf[...] = total.T.astype(BF16)

    def slot_copy(source, to):
        return pltpu.make_async_remote_copy(
            src_ref=z_buf.at[pl.ds(pl.multiple_of(to * HEAD, HEAD), HEAD), :],
            dst_ref=z_all.at[pl.ds(pl.multiple_of(source * HEAD, HEAD), HEAD), :],
            send_sem=zs.at[to],
            recv_sem=zr.at[source],
            device_id={"row": to},
            device_id_type=MESH,
        )

    for k in (4, 3, 5, 2, 6, 1, 7):
        slot_copy(me_r, lax.rem(me_r + k, rows_n)).start()
    own = pl.ds(pl.multiple_of(me_r * HEAD, HEAD), HEAD)
    z_all[own, :] = z_buf[own, :]

    @pl.loop(1, rows_n)
    def _(k):
        slot_copy(lax.rem(me_r + k, rows_n), me_r).wait_recv()

    got = jnp.concatenate([z_all[pl.ds(i * HEAD, HEAD), :] for i in range(rows_n)], axis=1)
    result = jnp.dot(got, expand[...], preferred_element_type=F32)
    wide = rows_n * q_dev
    tail = jnp.concatenate(
        [result[:TAIL, wide : wide + LANES], result[TAIL:, wide + LANES :]], axis=1
    )
    out[...] = jnp.concatenate([result[:, :wide], tail], axis=0).astype(BF16)

    @pl.loop(1, rows_n)
    def _(k):
        to = lax.rem(me_r + k, rows_n)
        for t in range(chunks):
            panel_copy(t, me_r, to).wait_send()
        slot_copy(me_r, to).wait_send()

    @pl.loop(1, cols_n)
    def _(k):
        partial_copy(me_c, lax.rem(me_c + k, cols_n)).wait_send()


def shards(panels, amplitudes, virt_coeff, row_owner):
    rows_n = lax.axis_size("row")
    cols_n = lax.axis_size("col")
    q_own, depth = panels.shape
    nao, virt = virt_coeff.shape
    q_dev = rows_n * q_own
    chunks = -(-depth // (BLOCKS * WIDTH))
    tall = BLOCKS * q_own
    padded = -(-nao // WIDTH) * WIDTH
    dense = q_dev + q_dev // 2
    vmem = pltpu.VMEM
    dma = pltpu.SemaphoreType.DMA
    return pl.pallas_call(
        functools.partial(kernel, rows_n, cols_n),
        out_shape=jax.ShapeDtypeStruct((HEAD + TAIL, rows_n * q_dev), BF16),
        in_specs=[pl.BlockSpec(memory_space=pl.ANY)] * 4,
        out_specs=pl.BlockSpec(memory_space=pltpu.VMEM),
        scratch_shapes=[
            vmem(amplitudes.shape, BF16),
            vmem((virt, nao), BF16),
            vmem(panels.shape, BF16),
            vmem((1, nao), jnp.int32),
            vmem((1, padded), jnp.int32),
            vmem((tall, chunks * WIDTH), F32),
            vmem((chunks, rows_n * tall, WIDTH), BF16),
            vmem((padded, LANES), F32),
            vmem((nao, cols_n // 2 * 3 * LANES), BF16),
            vmem((rows_n * LANES, 2 * rows_n * q_dev), BF16),
            vmem((cols_n, dense, LANES), F32),
            vmem((cols_n, dense, LANES), F32),
            vmem((rows_n * HEAD, LANES), BF16),
            vmem((rows_n * HEAD, LANES), BF16),
            dma((4,)),
            dma((chunks, rows_n)),
            dma((chunks, rows_n)),
            dma((cols_n,)),
            dma((cols_n,)),
            dma((rows_n,)),
            dma((rows_n,)),
        ],
        compiler_params=pltpu.CompilerParams(
            collective_id=0, has_side_effects=True, vmem_limit_bytes=56 * 1024 * 1024
        ),
        cost_estimate=pl.CostEstimate(
            flops=2 * virt * depth * LANES, bytes_accessed=amplitudes.size * 2, transcendentals=0
        ),
        name="density",
    )(panels, row_owner.reshape(1, nao), amplitudes, virt_coeff.T)


def solution(mesh):
    placed = (P(("aux", "row"), "col"), P("row", "col"), P(), P())
    return jax.shard_map(
        shards, mesh=mesh, in_specs=placed, out_specs=P(("row", "col"), "aux"), check_vma=False
    )
```

time: 176 us -> 32 us (0.18)
  waiting for transfers between devices: 88.9 us -> 0 us
  blocking collectives: 52.2 us -> 0 us
  Pallas kernels: 0 us -> 30.5 us
  between operations: 14.2 us -> 0.01 us
  matrix products: 10 us -> 0 us
  local copies, waits for them, and re-layouts: 9.38 us -> 1.31 us
    unnamed x2 -> x0, waiting for transfers between devices: 88.9 us -> none
    pallas_call x0 -> x1, Pallas kernels: none -> 30.5 us  [shards(): pl.pallas_call(functools.partial(kernel, rows_n, cols_n), out_shape=jax.S...]
    all_gather x1 -> x0, blocking collectives: 28.7 us -> none  [shards(): lax.all_gather(panels, 'row', axis=0, tiled=True)]
    all_to_all x1 -> x0, blocking collectives: 23.5 us -> none  [shards(): lax.all_to_all(outgoing.reshape(count, capacity * local_q * occ_dev), ('r...]
    dot_general x2 -> x0, matrix products: 10 us -> none  [the longest x1 6.08 us: shards(): lax.dot_general(lax.all_gather(panels, 'row', axis=0, tiled=True), amplit...]
    scatter x1 -> x0, local copies, waits for them, and re-layouts: 6.65 us -> none  [shards(): jnp.zeros((count * capacity, local_q * occ_dev), jnp.bfloat16).at[target]]
  transfers between devices with their start and end apart: 1 -> 0, of which waited for: 1 -> 0; matrix products, arithmetic and copies ran while one was open for 1% -> 0% of each run, Pallas kernels for 0% -> 0%
where the time goes in v2:
time: 32 us; the launch traced here: 31.9 us
  Pallas kernels  30.5 us (95%)
  local copies, waits for them, and re-layouts  1.31 us (4%)
    pallas_call x1, Pallas kernels, shards(): pl.pallas_call(functools.partial(kernel, rows_n, cols_n), out_shape=jax.S...  30.5 us
    unnamed x1, local copies, waits for them, and re-layouts  1.31 us

profile of v2, /device:TPU:8, one launch (start us, length us, event | category | flops | bytes accessed | tf_op | source)
XLA Modules:
  0.0 31.9 jit_solution(14077032559708491503)
XLA Ops:
  0.0 30.5 %density.1 = bf16[24,256]{1,0:T(8,128)(2,1)} custom-call(bf16[4,2700]{1,0:T(4,128)(2,1)} %panels.1, s32[1,1500]{1,0:T(1,128)} %bitcast.3, bf16[1350,2700]{1,0:T(8,128)(2,1)} %amp.1, bf16[1350,1500]{1,0:T(8,128)(2,1)} %bitcast.2), custom_call_target="tpu_custom_call" | custom-call | flops 933120000 | bytes 7290000 | tf_op jit(solution)/shard_map/density/pallas_call | solution.py:277
  30.6 1.3 %copy.6 = bf16[24,256]{1,0:T(8,128)(2,1)} copy(bf16[24,256]{1,0:T(8,128)(2,1)} %density.1) | data formatting | bytes 24576

commit v3 on v2

v3 whole, which is shorter than its diff:
```python
import functools
import jax
import jax.numpy as jnp
from jax import lax
from jax.experimental import pallas as pl
from jax.experimental.pallas import tpu as pltpu
from jax.sharding import PartitionSpec as P

F32 = jnp.float32
BF16 = jnp.bfloat16
MESH = pl.DeviceIdType.MESH
NT = (((1,), (1,)), ((), ()))

LANES = 128
BLOCKS = 4
WIDTH = 256
HEAD = 16
TAIL = 8
QUAD = 4


def split(x):
    hi = x.astype(BF16)
    lo = (x - hi.astype(F32)).astype(BF16)
    return jnp.concatenate([hi, lo], axis=0)


def iota(shape, dim):
    return lax.broadcasted_iota(jnp.int32, shape, dim)


def kernel(
    rows_n,
    cols_n,
    aux_n,
    panels,
    owner,
    amp,
    coeff_t,
    out,
    t_buf,
    w_buf,
    p_buf,
    o_buf,
    names,
    x_stage,
    x_all,
    place,
    spread,
    expand,
    d_buf,
    r_buf,
    z_buf,
    z_all,
    local_sem,
    xs,
    xr,
    ds,
    dr,
    zs,
    zr,
):
    me_r = lax.axis_index("row")
    me_c = lax.axis_index("col")
    me_a = lax.axis_index("aux")
    worker = me_a == aux_n - 1
    q_own, depth = panels.shape
    virt, nao = coeff_t.shape
    q_dev = rows_n * q_own
    q_all = aux_n * q_dev
    chunks = x_all.shape[0]
    block = chunks * WIDTH
    tall = BLOCKS * q_own
    count = rows_n * cols_n
    sources = aux_n * rows_n
    dense = q_dev + q_dev // 2
    pair = 3 * LANES
    order = (4, 3, 5, 2, 6, 1, 7)

    def row_at(k):
        return lax.rem(me_r + k, rows_n)

    barrier = pltpu.get_barrier_semaphore()

    def greet(**to):
        pl.semaphore_signal(barrier, inc=1, device_id=to, device_id_type=MESH)

    for k in order:
        greet(row=row_at(k), aux=aux_n - 1)

    cp_p = pltpu.make_async_copy(panels, p_buf, local_sem.at[0])
    cp_o = pltpu.make_async_copy(owner, o_buf, local_sem.at[1])
    cp_t = pltpu.make_async_copy(amp, t_buf, local_sem.at[2])
    cp_w = pltpu.make_async_copy(coeff_t, w_buf, local_sem.at[3])
    cp_p.start()

    @pl.when(worker)
    def _():
        for k in order + (0,):
            greet(row=row_at(k), aux=0)
        cp_o.start()
        cp_t.start()
        cp_w.start()
        for k in range(1, cols_n):
            greet(col=lax.rem(me_c + k, cols_n))

    @pl.when(jnp.logical_not(worker))
    def _():
        greet(aux=aux_n - 1)

    x_stage[...] = jnp.zeros_like(x_stage)
    cp_p.wait()
    for t in range(chunks):
        for kb in range(BLOCKS):
            start = (t * BLOCKS + kb) * WIDTH
            width = min(WIDTH, depth - start)
            if width > 0:
                x_stage[t, pl.ds(kb * q_own, q_own), pl.ds(0, width)] = p_buf[
                    :, pl.ds(start, width)
                ].astype(F32)
    me_source = me_a * rows_n + me_r
    for t in range(chunks):
        x_all[t, pl.ds(pl.multiple_of(me_source * tall, tall), tall), :] = x_stage[t].astype(BF16)

    def panel_copy(t, source, to):
        rows = x_all.at[t, pl.ds(pl.multiple_of(source * tall, tall), tall), :]
        return pltpu.make_async_remote_copy(
            src_ref=rows,
            dst_ref=rows,
            send_sem=xs.at[t, to],
            recv_sem=xr.at[t, source],
            device_id={"row": to, "aux": aux_n - 1},
            device_id_type=MESH,
        )

    def partial_copy(source, to):
        return pltpu.make_async_remote_copy(
            src_ref=d_buf.at[to],
            dst_ref=r_buf.at[source],
            send_sem=ds.at[to],
            recv_sem=dr.at[source],
            device_id={"col": to},
            device_id_type=MESH,
        )

    def slot_copy(source, to, aux):
        return pltpu.make_async_remote_copy(
            src_ref=z_buf.at[aux, pl.ds(pl.multiple_of(to * HEAD, HEAD), HEAD), :],
            dst_ref=z_all.at[pl.ds(pl.multiple_of(source * HEAD, HEAD), HEAD), :],
            send_sem=zs.at[aux, to],
            recv_sem=zr.at[source],
            device_id={"row": to, "aux": aux},
            device_id_type=MESH,
        )

    @pl.when(worker)
    def _():
        pl.semaphore_wait(barrier, sources - 1 + cols_n - 1)

    @pl.when(jnp.logical_not(worker))
    def _():
        pl.semaphore_wait(barrier, rows_n)

    for t in range(chunks):
        for k in order:
            panel_copy(t, me_source, row_at(k)).start()

        @pl.when(jnp.logical_not(worker))
        def _():
            panel_copy(t, me_source, me_r).start()

    for i in range(rows_n):
        a = iota((LANES, rows_n * q_dev), 0)
        n = iota((LANES, rows_n * q_dev), 1)
        head = jnp.where((a < q_dev) & (n == a * rows_n + i), 1.0, 0.0)
        tail = jnp.where(
            (a >= q_dev) & (a < dense) & (lax.rem(n, LANES) == (a - q_dev) * rows_n + i), 1.0, 0.0
        )
        expand[pl.ds(i * LANES, LANES), :] = jnp.concatenate([head, tail], axis=1).astype(BF16)

    @pl.when(worker)
    def _():
        names[...] = jnp.full_like(names, -1)
        cp_o.wait()
        names[:, pl.ds(0, nao)] = o_buf[...]
        tri = (iota((WIDTH, WIDTH), 0) < iota((WIDTH, WIDTH), 1)).astype(BF16)
        carry = jnp.zeros((count, 1), F32)
        for b in range(names.shape[1] // WIDTH):
            name = names[:, pl.ds(b * WIDTH, WIDTH)]
            ones = jnp.where(name == iota((count, WIDTH), 0), 1.0, 0.0).astype(F32)
            before = jnp.dot(ones.astype(BF16), tri, preferred_element_type=F32) + carry
            slot = jnp.sum(ones * before, axis=0, keepdims=True)
            carry = carry + jnp.sum(ones, axis=1, keepdims=True)
            at_row = lax.div(name, jnp.int32(cols_n))
            at_col = name - at_row * cols_n
            at_pair = lax.div(at_col, jnp.int32(2))
            odd = at_col - at_pair * 2
            base = (at_pair * pair + at_row * HEAD).astype(F32)
            early = base + (odd * LANES).astype(F32) + slot
            late = base + (odd * TAIL + (2 * LANES - HEAD)).astype(F32) + slot
            lane = jnp.where(slot < HEAD, early, late)
            lane = jnp.where(name < 0, -1.0, lane)
            place[pl.ds(b * WIDTH, WIDTH), :] = jnp.broadcast_to(lane, (LANES, WIDTH)).T

        @pl.loop(0, spread.shape[1] // LANES)
        def _(b):
            at = (iota((nao, LANES), 1) + b * LANES).astype(F32)
            hot = jnp.where(place[pl.ds(0, nao), :] == at, 1.0, 0.0)
            spread[:, pl.ds(pl.multiple_of(b * LANES, LANES), LANES)] = hot.astype(BF16)

        cp_t.wait()
        partial = jnp.zeros((q_all, virt), F32)
        for t in range(chunks):

            @pl.loop(1, sources)
            def _(k):
                panel_copy(t, lax.rem(me_source + k, sources), me_r).wait_recv()

            for kb in range(BLOCKS):
                start = (t * BLOCKS + kb) * WIDTH
                width = min(WIDTH, depth - start)
                if width <= 0:
                    continue
                wide = sources * tall
                q = iota((q_all, wide), 0)
                source = lax.div(q, q_own) * tall + kb * q_own + lax.rem(q, q_own)
                pick = jnp.where(source == iota((q_all, wide), 1), 1.0, 0.0).astype(BF16)
                g = jnp.dot(pick, x_all[t], preferred_element_type=F32).astype(BF16)
                partial = partial + lax.dot_general(
                    g[:, :width], t_buf[:, pl.ds(start, width)], NT, preferred_element_type=F32
                )

        cp_w.wait()
        half = jnp.dot(split(partial), w_buf[...], preferred_element_type=F32)
        half = split(half[:q_all] + half[q_all:])

        quads = cols_n // QUAD
        my_quad = lax.div(me_c, QUAD)
        lower = lax.rem(iota((q_dev // 2, LANES), 1), 2 * TAIL) < TAIL
        for step in range(quads):
            quad = lax.rem(my_quad + (2, 1, 3, 0)[step], quads)
            lanes = QUAD // 2 * pair
            part = spread[:, pl.ds(pl.multiple_of(quad * lanes, lanes), lanes)]
            slots = jnp.dot(half, part, preferred_element_type=F32)
            slots = slots[:q_all] + slots[q_all:]
            for j in range(QUAD):
                to = quad * QUAD + j
                first = j // 2 * pair
                for aux in range(aux_n):
                    rows = slots[aux * q_dev : (aux + 1) * q_dev]
                    head = rows[:, first + j % 2 * LANES : first + (j % 2 + 1) * LANES]
                    tail = rows[:, first + 2 * LANES : first + 3 * LANES]
                    upper_q, lower_q = tail[: q_dev // 2], tail[q_dev // 2 :]
                    if j % 2:
                        upper_q = pltpu.roll(upper_q, LANES - TAIL, 1)
                    else:
                        lower_q = pltpu.roll(lower_q, TAIL, 1)
                    d_buf[to, pl.ds(aux * dense, q_dev), :] = head
                    d_buf[to, pl.ds(aux * dense + q_dev, q_dev // 2), :] = jnp.where(
                        lower, upper_q, lower_q
                    )

                @pl.when(to != me_c)
                def _():
                    partial_copy(me_c, to).start()

        total = d_buf[me_c]
        for k in range(1, cols_n):
            source = lax.rem(me_c + k, cols_n)
            partial_copy(source, me_c).wait_recv()
            total = total + r_buf[source]
        for aux in range(aux_n):
            own = total[aux * dense : (aux + 1) * dense]
            own = jnp.concatenate([own, jnp.zeros((LANES - dense, LANES), F32)], axis=0)
            z_buf[aux] = own.T.astype(BF16)
            for k in order:
                slot_copy(me_r, row_at(k), aux).start()
            if aux < aux_n - 1:
                slot_copy(me_r, me_r, aux).start()
        own = pl.ds(pl.multiple_of(me_r * HEAD, HEAD), HEAD)
        z_all[own, :] = z_buf[aux_n - 1, own, :]

    @pl.loop(1, rows_n)
    def _(k):
        slot_copy(row_at(k), me_r, me_a).wait_recv()

    @pl.when(jnp.logical_not(worker))
    def _():
        slot_copy(me_r, me_r, me_a).wait_recv()

    got = jnp.concatenate([z_all[pl.ds(i * HEAD, HEAD), :] for i in range(rows_n)], axis=1)
    result = jnp.dot(got, expand[...], preferred_element_type=F32)
    wide = rows_n * q_dev
    tail = jnp.concatenate(
        [result[:TAIL, wide : wide + LANES], result[TAIL:, wide + LANES :]], axis=1
    )
    out[...] = jnp.concatenate([result[:, :wide], tail], axis=0)

    @pl.loop(1, rows_n)
    def _(k):
        for t in range(chunks):
            panel_copy(t, me_source, row_at(k)).wait_send()

    @pl.when(jnp.logical_not(worker))
    def _():
        for t in range(chunks):
            panel_copy(t, me_source, me_r).wait_send()

    @pl.when(worker)
    def _():
        @pl.loop(1, cols_n)
        def _(k):
            partial_copy(me_c, lax.rem(me_c + k, cols_n)).wait_send()

        for aux in range(aux_n):
            for k in order:
                slot_copy(me_r, row_at(k), aux).wait_send()
            if aux < aux_n - 1:
                slot_copy(me_r, me_r, aux).wait_send()


def shards(panels, amplitudes, virt_coeff, row_owner):
    rows_n = lax.axis_size("row")
    cols_n = lax.axis_size("col")
    aux_n = lax.axis_size("aux")
    q_own, depth = panels.shape
    nao, virt = virt_coeff.shape
    q_dev = rows_n * q_own
    chunks = -(-depth // (BLOCKS * WIDTH))
    tall = BLOCKS * q_own
    padded = -(-nao // WIDTH) * WIDTH
    dense = q_dev + q_dev // 2
    vmem = pltpu.VMEM
    dma = pltpu.SemaphoreType.DMA
    return pl.pallas_call(
        functools.partial(kernel, rows_n, cols_n, aux_n),
        out_shape=jax.ShapeDtypeStruct((HEAD + TAIL, rows_n * q_dev), F32),
        in_specs=[pl.BlockSpec(memory_space=pl.ANY)] * 4,
        out_specs=pl.BlockSpec(memory_space=pltpu.VMEM),
        scratch_shapes=[
            vmem(amplitudes.shape, BF16),
            vmem((virt, nao), BF16),
            vmem(panels.shape, BF16),
            vmem((1, nao), jnp.int32),
            vmem((1, padded), jnp.int32),
            vmem((chunks, tall, WIDTH), F32),
            vmem((chunks, aux_n * rows_n * tall, WIDTH), BF16),
            vmem((padded, LANES), F32),
            vmem((nao, cols_n // 2 * 3 * LANES), BF16),
            vmem((rows_n * LANES, 2 * rows_n * q_dev), BF16),
            vmem((cols_n, aux_n * dense, LANES), F32),
            vmem((cols_n, aux_n * dense, LANES), F32),
            vmem((aux_n, rows_n * HEAD, LANES), BF16),
            vmem((rows_n * HEAD, LANES), BF16),
            dma((4,)),
            dma((chunks, rows_n)),
            dma((chunks, aux_n * rows_n)),
            dma((cols_n,)),
            dma((cols_n,)),
            dma((aux_n, rows_n)),
            dma((rows_n,)),
        ],
        compiler_params=pltpu.CompilerParams(
            collective_id=0, has_side_effects=True, vmem_limit_bytes=56 * 1024 * 1024
        ),
        cost_estimate=pl.CostEstimate(
            flops=2 * virt * depth * LANES, bytes_accessed=amplitudes.size * 2, transcendentals=0
        ),
        name="density",
    )(panels, row_owner.reshape(1, nao), amplitudes, virt_coeff.T).astype(BF16)


def solution(mesh):
    placed = (P(("aux", "row"), "col"), P("row", "col"), P(), P())
    return jax.shard_map(
        shards, mesh=mesh, in_specs=placed, out_specs=P(("row", "col"), "aux"), check_vma=False
    )
```

time: 32 us -> 33.8 us (1.056)
  the two profiles are of different devices: /device:TPU:8 before, /device:TPU:1 now
where the time goes in v3:
time: 33.8 us; the launch traced here: 33.6 us
  Pallas kernels  32.2 us (95%)
  other arithmetic  1.34 us (4%)
    pallas_call x1, Pallas kernels, shards(): pl.pallas_call(functools.partial(kernel, rows_n, cols_n, aux_n), out_shap...  32.2 us
    convert_element_type x1, other arithmetic, shards(): return pl.pallas_call(functools.partial(kernel, rows_n, cols_n, aux_n), o...  1.34 us

profile of v3, /device:TPU:1, one launch (start us, length us, event | category | flops | bytes accessed | tf_op | source)
XLA Modules:
  0.0 33.6 jit_solution(5819846272330275516)
XLA Ops:
  0.0 32.2 %density.1 = f32[24,256]{1,0:T(8,128)} custom-call(bf16[4,2700]{1,0:T(4,128)(2,1)} %panels.1, s32[1,1500]{1,0:T(1,128)} %bitcast.3, bf16[1350,2700]{1,0:T(8,128)(2,1)} %amp.1, bf16[1350,1500]{1,0:T(8,128)(2,1)} %bitcast.2), custom_call_target="tpu_custom_call" | custom-call | flops 933120000 | bytes 7290000 | tf_op jit(solution)/shard_map/density/pallas_call | solution.py:335
  32.2 1.3 %convert_element_type.3 = bf16[24,256]{1,0:T(8,128)(2,1)} convert(f32[24,256]{1,0:T(8,128)} %density.1) | non-fusion elementwise | flops 6144 | bytes 36864 | tf_op jit(solution)/shard_map/convert_element_type | solution.py:370

commit v4 on v2

--- a/solution.py
+++ b/solution.py
@@ -61,25 +61,31 @@
 ):
     me_r = lax.axis_index("row")
     me_c = lax.axis_index("col")
+    me_a = lax.axis_index("aux")
     q_own, depth = panels.shape
     virt, nao = coeff_t.shape
     q_dev = rows_n * q_own
     chunks = x_all.shape[0]
-    block = chunks * WIDTH
     tall = BLOCKS * q_own
     count = rows_n * cols_n
     dense = q_dev + q_dev // 2
     pair = 3 * LANES
+    order = (4, 3, 5, 2, 6, 1, 7)
+    far = (10, 6, 9, 11, 5, 7, 8, 2, 14, 13, 15, 12, 4, 3, 1)
+
+    def row_at(k):
+        return lax.rem(me_r + k, rows_n)
 
     barrier = pltpu.get_barrier_semaphore()
-    for k in range(1, rows_n):
-        pl.semaphore_signal(
-            barrier, inc=1, device_id={"row": lax.rem(me_r + k, rows_n)}, device_id_type=MESH
-        )
-    for k in range(1, cols_n):
-        pl.semaphore_signal(
-            barrier, inc=1, device_id={"col": lax.rem(me_c + k, cols_n)}, device_id_type=MESH
-        )
+    def greet(**to):
+        pl.semaphore_signal(barrier, inc=1, device_id=to, device_id_type=MESH)
+
+    for k in order:
+        greet(row=row_at(k))
+    for k in order + (0,):
+        greet(row=row_at(k), aux=1 - me_a)
+    for k in far:
+        greet(col=lax.rem(me_c + k, cols_n), aux=1 - me_a)
     cp_p = pltpu.make_async_copy(panels, p_buf, local_sem.at[0])
     cp_o = pltpu.make_async_copy(owner, o_buf, local_sem.at[1])
     cp_t = pltpu.make_async_copy(amp, t_buf, local_sem.at[2])
@@ -91,16 +97,19 @@
 
     x_stage[...] = jnp.zeros_like(x_stage)
     cp_p.wait()
-    for kb in range(BLOCKS):
-        width = min(block, depth - kb * block)
-        x_stage[pl.ds(kb * q_own, q_own), pl.ds(0, width)] = p_buf[
-            :, pl.ds(kb * block, width)
-        ].astype(F32)
+    for t in range(chunks):
+        for kb in range(BLOCKS):
+            start = (t * BLOCKS + kb) * WIDTH
+            width = min(WIDTH, depth - start)
+            if width > 0:
+                x_stage[t, pl.ds(kb * q_own, q_own), pl.ds(0, width)] = p_buf[
+                    :, pl.ds(start, width)
+                ].astype(F32)
     own_rows = pl.ds(pl.multiple_of(me_r * tall, tall), tall)
     for t in range(chunks):
-        x_all[t, own_rows, :] = x_stage[:, pl.ds(t * WIDTH, WIDTH)].astype(BF16)
-
-    pl.semaphore_wait(barrier, rows_n - 1 + cols_n - 1)
+        x_all[t, own_rows, :] = x_stage[t].astype(BF16)
+
+    pl.semaphore_wait(barrier, 2 * (rows_n - 1) + cols_n)
 
     def panel_copy(t, source, to):
         rows = x_all.at[t, pl.ds(pl.multiple_of(source * tall, tall), tall), :]
@@ -114,8 +123,8 @@
         )
 
     for t in range(chunks):
-        for k in (4, 3, 5, 2, 6, 1, 7):
-            panel_copy(t, me_r, lax.rem(me_r + k, rows_n)).start()
+        for k in order:
+            panel_copy(t, me_r, row_at(k)).start()
 
     names[...] = jnp.full_like(names, -1)
     cp_o.wait()
@@ -163,7 +172,7 @@
             panel_copy(t, lax.rem(me_r + k, rows_n), me_r).wait_recv()
 
         for kb in range(BLOCKS):
-            start = kb * block + t * WIDTH
+            start = (t * BLOCKS + kb) * WIDTH
             width = min(WIDTH, depth - start)
             if width <= 0:
                 continue
@@ -185,7 +194,7 @@
             dst_ref=r_buf.at[source],
             send_sem=ds.at[to],
             recv_sem=dr.at[source],
-            device_id={"col": to},
+            device_id={"col": to, "aux": 1 - me_a},
             device_id_type=MESH,
         )
 
@@ -210,13 +219,10 @@
                 lower_q = pltpu.roll(lower_q, TAIL, 1)
             d_buf[to, pl.ds(0, q_dev), :] = head
             d_buf[to, pl.ds(q_dev, q_dev // 2), :] = jnp.where(lower, upper_q, lower_q)
-
-            @pl.when(to != me_c)
-            def _():
-                partial_copy(me_c, to).start()
-
-    total = d_buf[me_c]
-    for k in range(1, cols_n):
+            partial_copy(me_c, to).start()
+
+    total = jnp.zeros((dense, LANES), F32)
+    for k in (0,) + far[::-1]:
         source = lax.rem(me_c + k, cols_n)
         partial_copy(source, me_c).wait_recv()
         total = total + r_buf[source]
@@ -229,18 +235,16 @@
             dst_ref=z_all.at[pl.ds(pl.multiple_of(source * HEAD, HEAD), HEAD), :],
             send_sem=zs.at[to],
             recv_sem=zr.at[source],
-            device_id={"row": to},
+            device_id={"row": to, "aux": 1 - me_a},
             device_id_type=MESH,
         )
 
-    for k in (4, 3, 5, 2, 6, 1, 7):
-        slot_copy(me_r, lax.rem(me_r + k, rows_n)).start()
-    own = pl.ds(pl.multiple_of(me_r * HEAD, HEAD), HEAD)
-    z_all[own, :] = z_buf[own, :]
-
-    @pl.loop(1, rows_n)
+    for k in order + (0,):
+        slot_copy(me_r, row_at(k)).start()
+
+    @pl.loop(0, rows_n)
     def _(k):
-        slot_copy(lax.rem(me_r + k, rows_n), me_r).wait_recv()
+        slot_copy(row_at(k), me_r).wait_recv()
 
     got = jnp.concatenate([z_all[pl.ds(i * HEAD, HEAD), :] for i in range(rows_n)], axis=1)
     result = jnp.dot(got, expand[...], preferred_element_type=F32)
@@ -252,14 +256,16 @@
 
     @pl.loop(1, rows_n)
     def _(k):
-        to = lax.rem(me_r + k, rows_n)
         for t in range(chunks):
-            panel_copy(t, me_r, to).wait_send()
+            panel_copy(t, me_r, row_at(k)).wait_send()
+
+    @pl.loop(0, cols_n)
+    def _(to):
+        partial_copy(me_c, to).wait_send()
+
+    @pl.loop(0, rows_n)
+    def _(to):
         slot_copy(me_r, to).wait_send()
-
-    @pl.loop(1, cols_n)
-    def _(k):
-        partial_copy(me_c, lax.rem(me_c + k, cols_n)).wait_send()
 
 
 def shards(panels, amplitudes, virt_coeff, row_owner):
@@ -276,7 +282,7 @@
     dma = pltpu.SemaphoreType.DMA
     return pl.pallas_call(
         functools.partial(kernel, rows_n, cols_n),
-        out_shape=jax.ShapeDtypeStruct((HEAD + TAIL, rows_n * q_dev), BF16),
+        out_shape=pltpu.VMEM((HEAD + TAIL, rows_n * q_dev), BF16),
         in_specs=[pl.BlockSpec(memory_space=pl.ANY)] * 4,
         out_specs=pl.BlockSpec(memory_space=pltpu.VMEM),
         scratch_shapes=[
@@ -285,7 +291,7 @@
             vmem(panels.shape, BF16),
             vmem((1, nao), jnp.int32),
             vmem((1, padded), jnp.int32),
-            vmem((tall, chunks * WIDTH), F32),
+            vmem((chunks, tall, WIDTH), F32),
             vmem((chunks, rows_n * tall, WIDTH), BF16),
             vmem((padded, LANES), F32),
             vmem((nao, cols_n // 2 * 3 * LANES), BF16),

time: 32 us -> 32.4 us (1.012)
  the two profiles are of different devices: /device:TPU:8 before, /device:TPU:1 now
where the time goes in v4:
time: 32.4 us; the launch traced here: 32.3 us
  Pallas kernels  31.7 us (98%)
  local copies, waits for them, and re-layouts  0.6 us (2%)
    pallas_call x1, Pallas kernels, shards(): pl.pallas_call(functools.partial(kernel, rows_n, cols_n), out_shape=pltpu...  31.7 us

profile of v4, /device:TPU:1, one launch (start us, length us, event | category | flops | bytes accessed | tf_op | source)
XLA Modules:
  0.0 32.3 jit_solution(16007202208508796057)
XLA Ops:
  0.0 31.7 %density.1 = bf16[24,256]{1,0:T(8,128)(2,1)S(1)} custom-call(bf16[4,2700]{1,0:T(4,128)(2,1)} %panels.1, s32[1,1500]{1,0:T(1,128)} %bitcast.3, bf16[1350,2700]{1,0:T(8,128)(2,1)} %amp.1, bf16[1350,1500]{1,0:T(8,128)(2,1)} %bitcast.2), custom_call_target="tpu_custom_call" | custom-call | flops 933120000 | bytes 7290000 | tf_op jit(solution)/shard_map/density/pallas_call | solution.py:283
  31.7 0.6 %copy.6 = bf16[24,256]{1,0:T(8,128)(2,1)} copy(bf16[24,256]{1,0:T(8,128)(2,1)S(1)} %density.1) | data formatting | bytes 24576

commit v5 on v4

--- a/solution.py
+++ b/solution.py
@@ -61,7 +61,6 @@
 ):
     me_r = lax.axis_index("row")
     me_c = lax.axis_index("col")
-    me_a = lax.axis_index("aux")
     q_own, depth = panels.shape
     virt, nao = coeff_t.shape
     q_dev = rows_n * q_own
@@ -82,10 +81,8 @@
 
     for k in order:
         greet(row=row_at(k))
-    for k in order + (0,):
-        greet(row=row_at(k), aux=1 - me_a)
     for k in far:
-        greet(col=lax.rem(me_c + k, cols_n), aux=1 - me_a)
+        greet(col=lax.rem(me_c + k, cols_n))
     cp_p = pltpu.make_async_copy(panels, p_buf, local_sem.at[0])
     cp_o = pltpu.make_async_copy(owner, o_buf, local_sem.at[1])
     cp_t = pltpu.make_async_copy(amp, t_buf, local_sem.at[2])
@@ -109,7 +106,7 @@
     for t in range(chunks):
         x_all[t, own_rows, :] = x_stage[t].astype(BF16)
 
-    pl.semaphore_wait(barrier, 2 * (rows_n - 1) + cols_n)
+    pl.semaphore_wait(barrier, rows_n - 1 + cols_n - 1)
 
     def panel_copy(t, source, to):
         rows = x_all.at[t, pl.ds(pl.multiple_of(source * tall, tall), tall), :]
@@ -194,7 +191,7 @@
             dst_ref=r_buf.at[source],
             send_sem=ds.at[to],
             recv_sem=dr.at[source],
-            device_id={"col": to, "aux": 1 - me_a},
+            device_id={"col": to},
             device_id_type=MESH,
         )
 
@@ -219,10 +216,13 @@
                 lower_q = pltpu.roll(lower_q, TAIL, 1)
             d_buf[to, pl.ds(0, q_dev), :] = head
             d_buf[to, pl.ds(q_dev, q_dev // 2), :] = jnp.where(lower, upper_q, lower_q)
-            partial_copy(me_c, to).start()
-
-    total = jnp.zeros((dense, LANES), F32)
-    for k in (0,) + far[::-1]:
+        for k in (2, 1, 3, 0):
+            to = quad * QUAD + lax.rem(me_c + k, QUAD)
+            if step < quads - 1 or k:
+                partial_copy(me_c, to).start()
+
+    total = d_buf[me_c]
+    for k in far[::-1]:
         source = lax.rem(me_c + k, cols_n)
         partial_copy(source, me_c).wait_recv()
         total = total + r_buf[source]
@@ -235,14 +235,16 @@
             dst_ref=z_all.at[pl.ds(pl.multiple_of(source * HEAD, HEAD), HEAD), :],
             send_sem=zs.at[to],
             recv_sem=zr.at[source],
-            device_id={"row": to, "aux": 1 - me_a},
+            device_id={"row": to},
             device_id_type=MESH,
         )
 
-    for k in order + (0,):
+    for k in order:
         slot_copy(me_r, row_at(k)).start()
-
-    @pl.loop(0, rows_n)
+    own = pl.ds(pl.multiple_of(me_r * HEAD, HEAD), HEAD)
+    z_all[own, :] = z_buf[own, :]
+
+    @pl.loop(1, rows_n)
     def _(k):
         slot_copy(row_at(k), me_r).wait_recv()
 
@@ -258,14 +260,11 @@
     def _(k):
         for t in range(chunks):
             panel_copy(t, me_r, row_at(k)).wait_send()
-
-    @pl.loop(0, cols_n)
-    def _(to):
-        partial_copy(me_c, to).wait_send()
-
-    @pl.loop(0, rows_n)
-    def _(to):
-        slot_copy(me_r, to).wait_send()
+        slot_copy(me_r, row_at(k)).wait_send()
+
+    @pl.loop(1, cols_n)
+    def _(k):
+        partial_copy(me_c, lax.rem(me_c + k, cols_n)).wait_send()
 
 
 def shards(panels, amplitudes, virt_coeff, row_owner):

time: 32.4 us -> 30.9 us (0.954)
  the two profiles are of different devices: /device:TPU:1 before, /device:TPU:8 now
where the time goes in v5:
time: 30.9 us; the launch traced here: 30.8 us
  Pallas kernels  30.2 us (98%)
  local copies, waits for them, and re-layouts  0.6 us (2%)
    pallas_call x1, Pallas kernels, shards(): pl.pallas_call(functools.partial(kernel, rows_n, cols_n), out_shape=pltpu...  30.2 us

profile of v5, /device:TPU:8, one launch (start us, length us, event | category | flops | bytes accessed | tf_op | source)
XLA Modules:
  0.0 30.8 jit_solution(12472943090650508623)
XLA Ops:
  0.0 30.2 %density.1 = bf16[24,256]{1,0:T(8,128)(2,1)S(1)} custom-call(bf16[4,2700]{1,0:T(4,128)(2,1)} %panels.1, s32[1,1500]{1,0:T(1,128)} %bitcast.3, bf16[1350,2700]{1,0:T(8,128)(2,1)} %amp.1, bf16[1350,1500]{1,0:T(8,128)(2,1)} %bitcast.2), custom_call_target="tpu_custom_call" | custom-call | flops 933120000 | bytes 7290000 | tf_op jit(solution)/shard_map/density/pallas_call | solution.py:282
  30.2 0.6 %copy.6 = bf16[24,256]{1,0:T(8,128)(2,1)} copy(bf16[24,256]{1,0:T(8,128)(2,1)S(1)} %density.1) | data formatting | bytes 24576

commit v6 on v5

--- a/solution.py
+++ b/solution.py
@@ -9,7 +9,6 @@
 F32 = jnp.float32
 BF16 = jnp.bfloat16
 MESH = pl.DeviceIdType.MESH
-NT = (((1,), (1,)), ((), ()))
 
 LANES = 128
 BLOCKS = 4
@@ -38,6 +37,7 @@
     coeff_t,
     out,
     t_buf,
+    tt_buf,
     w_buf,
     p_buf,
     o_buf,
@@ -81,8 +81,6 @@
 
     for k in order:
         greet(row=row_at(k))
-    for k in far:
-        greet(col=lax.rem(me_c + k, cols_n))
     cp_p = pltpu.make_async_copy(panels, p_buf, local_sem.at[0])
     cp_o = pltpu.make_async_copy(owner, o_buf, local_sem.at[1])
     cp_t = pltpu.make_async_copy(amp, t_buf, local_sem.at[2])
@@ -90,38 +88,8 @@
     cp_p.start()
     cp_o.start()
     cp_t.start()
-    cp_w.start()
-
-    x_stage[...] = jnp.zeros_like(x_stage)
-    cp_p.wait()
-    for t in range(chunks):
-        for kb in range(BLOCKS):
-            start = (t * BLOCKS + kb) * WIDTH
-            width = min(WIDTH, depth - start)
-            if width > 0:
-                x_stage[t, pl.ds(kb * q_own, q_own), pl.ds(0, width)] = p_buf[
-                    :, pl.ds(start, width)
-                ].astype(F32)
-    own_rows = pl.ds(pl.multiple_of(me_r * tall, tall), tall)
-    for t in range(chunks):
-        x_all[t, own_rows, :] = x_stage[t].astype(BF16)
-
-    pl.semaphore_wait(barrier, rows_n - 1 + cols_n - 1)
-
-    def panel_copy(t, source, to):
-        rows = x_all.at[t, pl.ds(pl.multiple_of(source * tall, tall), tall), :]
-        return pltpu.make_async_remote_copy(
-            src_ref=rows,
-            dst_ref=rows,
-            send_sem=xs.at[t, to],
-            recv_sem=xr.at[t, source],
-            device_id={"row": to},
-            device_id_type=MESH,
-        )
-
-    for t in range(chunks):
-        for k in order:
-            panel_copy(t, me_r, row_at(k)).start()
+    for k in far:
+        greet(col=lax.rem(me_c + k, cols_n))
 
     names[...] = jnp.full_like(names, -1)
     cp_o.wait()
@@ -151,6 +119,43 @@
         hot = jnp.where(place[pl.ds(0, nao), :] == at, 1.0, 0.0)
         spread[:, pl.ds(pl.multiple_of(b * LANES, LANES), LANES)] = hot.astype(BF16)
 
+    x_stage[...] = jnp.zeros_like(x_stage)
+    cp_p.wait()
+    for t in range(chunks):
+        for kb in range(BLOCKS):
+            start = (t * BLOCKS + kb) * WIDTH
+            width = min(WIDTH, depth - start)
+            if width > 0:
+                x_stage[t, pl.ds(kb * q_own, q_own), pl.ds(0, width)] = p_buf[
+                    :, pl.ds(start, width)
+                ].astype(F32)
+    own_rows = pl.ds(pl.multiple_of(me_r * tall, tall), tall)
+    for t in range(chunks):
+        x_all[t, own_rows, :] = x_stage[t].astype(BF16)
+
+    pl.semaphore_wait(barrier, rows_n - 1 + cols_n - 1)
+
+    def panel_copy(t, source, to):
+        rows = x_all.at[t, pl.ds(pl.multiple_of(source * tall, tall), tall), :]
+        return pltpu.make_async_remote_copy(
+            src_ref=rows,
+            dst_ref=rows,
+            send_sem=xs.at[t],
+            recv_sem=xr.at[t],
+            device_id={"row": to},
+            device_id_type=MESH,
+        )
+
+    for t in range(chunks):
+        for k in order:
+            panel_copy(t, me_r, row_at(k)).start()
+
+    cp_t.wait()
+    cp_w.start()
+    for k in range(0, depth, WIDTH):
+        width = min(WIDTH, depth - k)
+        tt_buf[pl.ds(k, width), :] = t_buf[:, pl.ds(k, width)].T
+
     for i in range(rows_n):
         a = iota((LANES, rows_n * q_dev), 0)
         n = iota((LANES, rows_n * q_dev), 1)
@@ -160,14 +165,10 @@
         )
         expand[pl.ds(i * LANES, LANES), :] = jnp.concatenate([head, tail], axis=1).astype(BF16)
 
-    cp_t.wait()
     partial = jnp.zeros((q_dev, virt), F32)
     for t in range(chunks):
-
-        @pl.loop(1, rows_n)
-        def _(k):
-            panel_copy(t, lax.rem(me_r + k, rows_n), me_r).wait_recv()
-
+        others = x_all.at[t, pl.ds(0, (rows_n - 1) * tall), :]
+        pltpu.make_async_copy(others, others, xr.at[t]).wait()
         for kb in range(BLOCKS):
             start = (t * BLOCKS + kb) * WIDTH
             width = min(WIDTH, depth - start)
@@ -177,8 +178,8 @@
             source = lax.div(q, q_own) * tall + kb * q_own + lax.rem(q, q_own)
             pick = jnp.where(source == iota((q_dev, LANES), 1), 1.0, 0.0).astype(BF16)
             g = jnp.dot(pick, x_all[t], preferred_element_type=F32).astype(BF16)
-            partial = partial + lax.dot_general(
-                g[:, :width], t_buf[:, pl.ds(start, width)], NT, preferred_element_type=F32
+            partial = partial + jnp.dot(
+                g[:, :width], tt_buf[pl.ds(start, width), :], preferred_element_type=F32
             )
 
     cp_w.wait()
@@ -189,8 +190,8 @@
         return pltpu.make_async_remote_copy(
             src_ref=d_buf.at[to],
             dst_ref=r_buf.at[source],
-            send_sem=ds.at[to],
-            recv_sem=dr.at[source],
+            send_sem=ds.at[0],
+            recv_sem=dr.at[0],
             device_id={"col": to},
             device_id_type=MESH,
         )
@@ -221,11 +222,14 @@
             if step < quads - 1 or k:
                 partial_copy(me_c, to).start()
 
+    for t in range(chunks):
+        sent = x_all.at[t, pl.ds(0, (rows_n - 1) * tall), :]
+        pltpu.make_async_copy(sent, sent, xs.at[t]).wait()
+    others = r_buf.at[pl.ds(0, cols_n - 1)]
+    pltpu.make_async_copy(others, others, dr.at[0]).wait()
     total = d_buf[me_c]
-    for k in far[::-1]:
-        source = lax.rem(me_c + k, cols_n)
-        partial_copy(source, me_c).wait_recv()
-        total = total + r_buf[source]
+    for k in range(1, cols_n):
+        total = total + r_buf[lax.rem(me_c + k, cols_n)]
     total = jnp.concatenate([total, jnp.zeros((LANES - dense, LANES), F32)], axis=0)
     z_buf[...] = total.T.astype(BF16)
 
@@ -233,8 +237,8 @@
         return pltpu.make_async_remote_copy(
             src_ref=z_buf.at[pl.ds(pl.multiple_of(to * HEAD, HEAD), HEAD), :],
             dst_ref=z_all.at[pl.ds(pl.multiple_of(source * HEAD, HEAD), HEAD), :],
-            send_sem=zs.at[to],
-            recv_sem=zr.at[source],
+            send_sem=zs.at[0],
+            recv_sem=zr.at[0],
             device_id={"row": to},
             device_id_type=MESH,
         )
@@ -244,9 +248,11 @@
     own = pl.ds(pl.multiple_of(me_r * HEAD, HEAD), HEAD)
     z_all[own, :] = z_buf[own, :]
 
-    @pl.loop(1, rows_n)
-    def _(k):
-        slot_copy(row_at(k), me_r).wait_recv()
+    partials_sent = d_buf.at[pl.ds(0, cols_n - 1)]
+    pltpu.make_async_copy(partials_sent, partials_sent, ds.at[0]).wait()
+
+    others = z_all.at[pl.ds(0, (rows_n - 1) * HEAD), :]
+    pltpu.make_async_copy(others, others, zr.at[0]).wait()
 
     got = jnp.concatenate([z_all[pl.ds(i * HEAD, HEAD), :] for i in range(rows_n)], axis=1)
     result = jnp.dot(got, expand[...], preferred_element_type=F32)
@@ -256,15 +262,8 @@
     )
     out[...] = jnp.concatenate([result[:, :wide], tail], axis=0).astype(BF16)
 
-    @pl.loop(1, rows_n)
-    def _(k):
-        for t in range(chunks):
-            panel_copy(t, me_r, row_at(k)).wait_send()
-        slot_copy(me_r, row_at(k)).wait_send()
-
-    @pl.loop(1, cols_n)
-    def _(k):
-        partial_copy(me_c, lax.rem(me_c + k, cols_n)).wait_send()
+    slots_sent = z_buf.at[pl.ds(0, (rows_n - 1) * HEAD), :]
+    pltpu.make_async_copy(slots_sent, slots_sent, zs.at[0]).wait()
 
 
 def shards(panels, amplitudes, virt_coeff, row_owner):
@@ -286,6 +285,7 @@
         out_specs=pl.BlockSpec(memory_space=pltpu.VMEM),
         scratch_shapes=[
             vmem(amplitudes.shape, BF16),
+            vmem((depth, virt), BF16),
             vmem((virt, nao), BF16),
             vmem(panels.shape, BF16),
             vmem((1, nao), jnp.int32),
@@ -300,12 +300,12 @@
             vmem((rows_n * HEAD, LANES), BF16),
             vmem((rows_n * HEAD, LANES), BF16),
             dma((4,)),
-            dma((chunks, rows_n)),
-            dma((chunks, rows_n)),
-            dma((cols_n,)),
-            dma((cols_n,)),
-            dma((rows_n,)),
-            dma((rows_n,)),
+            dma((chunks,)),
+            dma((chunks,)),
+            dma((1,)),
+            dma((1,)),
+            dma((1,)),
+            dma((1,)),
         ],
         compiler_params=pltpu.CompilerParams(
             collective_id=0, has_side_effects=True, vmem_limit_bytes=56 * 1024 * 1024

time: 30.9 us -> 30.3 us (0.981)
  Pallas kernels: 30.2 us -> 29.6 us
    pallas_call x1, Pallas kernels: 30.2 us -> 29.6 us  [shards(): pl.pallas_call(functools.partial(kernel, rows_n, cols_n), out_shape=pltpu...]
where the time goes in v6:
time: 30.3 us; the launch traced here: 30.2 us
  Pallas kernels  29.6 us (98%)
  local copies, waits for them, and re-layouts  0.6 us (2%)
    pallas_call x1, Pallas kernels, shards(): pl.pallas_call(functools.partial(kernel, rows_n, cols_n), out_shape=pltpu...  29.6 us

profile of v6, /device:TPU:8, one launch (start us, length us, event | category | flops | bytes accessed | tf_op | source)
XLA Modules:
  0.0 30.2 jit_solution(14636230661811704753)
XLA Ops:
  0.0 29.6 %density.1 = bf16[24,256]{1,0:T(8,128)(2,1)S(1)} custom-call(bf16[4,2700]{1,0:T(4,128)(2,1)} %panels.1, s32[1,1500]{1,0:T(1,128)} %bitcast.3, bf16[1350,2700]{1,0:T(8,128)(2,1)} %amp.1, bf16[1350,1500]{1,0:T(8,128)(2,1)} %bitcast.2), custom_call_target="tpu_custom_call" | custom-call | flops 933120000 | bytes 7290000 | tf_op jit(solution)/shard_map/density/pallas_call | solution.py:281
  29.6 0.6 %copy.6 = bf16[24,256]{1,0:T(8,128)(2,1)} copy(bf16[24,256]{1,0:T(8,128)(2,1)S(1)} %density.1) | data formatting | bytes 24576

commit v7 on v5

--- a/solution.py
+++ b/solution.py
@@ -81,8 +81,6 @@
 
     for k in order:
         greet(row=row_at(k))
-    for k in far:
-        greet(col=lax.rem(me_c + k, cols_n))
     cp_p = pltpu.make_async_copy(panels, p_buf, local_sem.at[0])
     cp_o = pltpu.make_async_copy(owner, o_buf, local_sem.at[1])
     cp_t = pltpu.make_async_copy(amp, t_buf, local_sem.at[2])
@@ -91,6 +89,8 @@
     cp_o.start()
     cp_t.start()
     cp_w.start()
+    for k in far:
+        greet(col=lax.rem(me_c + k, cols_n))
 
     x_stage[...] = jnp.zeros_like(x_stage)
     cp_p.wait()
@@ -113,8 +113,8 @@
         return pltpu.make_async_remote_copy(
             src_ref=rows,
             dst_ref=rows,
-            send_sem=xs.at[t, to],
-            recv_sem=xr.at[t, source],
+            send_sem=xs.at[t],
+            recv_sem=xr.at[t],
             device_id={"row": to},
             device_id_type=MESH,
         )
@@ -163,11 +163,8 @@
     cp_t.wait()
     partial = jnp.zeros((q_dev, virt), F32)
     for t in range(chunks):
-
-        @pl.loop(1, rows_n)
-        def _(k):
-            panel_copy(t, lax.rem(me_r + k, rows_n), me_r).wait_recv()
-
+        others = x_all.at[t, pl.ds(0, (rows_n - 1) * tall), :]
+        pltpu.make_async_copy(others, others, xr.at[t]).wait()
         for kb in range(BLOCKS):
             start = (t * BLOCKS + kb) * WIDTH
             width = min(WIDTH, depth - start)
@@ -189,8 +186,8 @@
         return pltpu.make_async_remote_copy(
             src_ref=d_buf.at[to],
             dst_ref=r_buf.at[source],
-            send_sem=ds.at[to],
-            recv_sem=dr.at[source],
+            send_sem=ds.at[0],
+            recv_sem=dr.at[0],
             device_id={"col": to},
             device_id_type=MESH,
         )
@@ -221,11 +218,14 @@
             if step < quads - 1 or k:
                 partial_copy(me_c, to).start()
 
+    for t in range(chunks):
+        sent = x_all.at[t, pl.ds(0, (rows_n - 1) * tall), :]
+        pltpu.make_async_copy(sent, sent, xs.at[t]).wait()
+    others = r_buf.at[pl.ds(0, cols_n - 1)]
+    pltpu.make_async_copy(others, others, dr.at[0]).wait()
     total = d_buf[me_c]
-    for k in far[::-1]:
-        source = lax.rem(me_c + k, cols_n)
-        partial_copy(source, me_c).wait_recv()
-        total = total + r_buf[source]
+    for k in range(1, cols_n):
+        total = total + r_buf[lax.rem(me_c + k, cols_n)]
     total = jnp.concatenate([total, jnp.zeros((LANES - dense, LANES), F32)], axis=0)
     z_buf[...] = total.T.astype(BF16)
 
@@ -233,8 +233,8 @@
         return pltpu.make_async_remote_copy(
             src_ref=z_buf.at[pl.ds(pl.multiple_of(to * HEAD, HEAD), HEAD), :],
             dst_ref=z_all.at[pl.ds(pl.multiple_of(source * HEAD, HEAD), HEAD), :],
-            send_sem=zs.at[to],
-            recv_sem=zr.at[source],
+            send_sem=zs.at[0],
+            recv_sem=zr.at[0],
             device_id={"row": to},
             device_id_type=MESH,
         )
@@ -244,9 +244,11 @@
     own = pl.ds(pl.multiple_of(me_r * HEAD, HEAD), HEAD)
     z_all[own, :] = z_buf[own, :]
 
-    @pl.loop(1, rows_n)
-    def _(k):
-        slot_copy(row_at(k), me_r).wait_recv()
+    partials_sent = d_buf.at[pl.ds(0, cols_n - 1)]
+    pltpu.make_async_copy(partials_sent, partials_sent, ds.at[0]).wait()
+
+    others = z_all.at[pl.ds(0, (rows_n - 1) * HEAD), :]
+    pltpu.make_async_copy(others, others, zr.at[0]).wait()
 
     got = jnp.concatenate([z_all[pl.ds(i * HEAD, HEAD), :] for i in range(rows_n)], axis=1)
     result = jnp.dot(got, expand[...], preferred_element_type=F32)
@@ -256,15 +258,8 @@
     )
     out[...] = jnp.concatenate([result[:, :wide], tail], axis=0).astype(BF16)
 
-    @pl.loop(1, rows_n)
-    def _(k):
-        for t in range(chunks):
-            panel_copy(t, me_r, row_at(k)).wait_send()
-        slot_copy(me_r, row_at(k)).wait_send()
-
-    @pl.loop(1, cols_n)
-    def _(k):
-        partial_copy(me_c, lax.rem(me_c + k, cols_n)).wait_send()
+    slots_sent = z_buf.at[pl.ds(0, (rows_n - 1) * HEAD), :]
+    pltpu.make_async_copy(slots_sent, slots_sent, zs.at[0]).wait()
 
 
 def shards(panels, amplitudes, virt_coeff, row_owner):
@@ -300,12 +295,12 @@
             vmem((rows_n * HEAD, LANES), BF16),
             vmem((rows_n * HEAD, LANES), BF16),
             dma((4,)),
-            dma((chunks, rows_n)),
-            dma((chunks, rows_n)),
-            dma((cols_n,)),
-            dma((cols_n,)),
-            dma((rows_n,)),
-            dma((rows_n,)),
+            dma((chunks,)),
+            dma((chunks,)),
+            dma((1,)),
+            dma((1,)),
+            dma((1,)),
+            dma((1,)),
         ],
         compiler_params=pltpu.CompilerParams(
             collective_id=0, has_side_effects=True, vmem_limit_bytes=56 * 1024 * 1024

time: 30.9 us -> 29.8 us (0.964)
  Pallas kernels: 30.2 us -> 29.1 us
    pallas_call x1, Pallas kernels: 30.2 us -> 29.1 us  [shards(): pl.pallas_call(functools.partial(kernel, rows_n, cols_n), out_shape=pltpu...]
where the time goes in v7:
time: 29.8 us; the launch traced here: 29.7 us
  Pallas kernels  29.1 us (98%)
  local copies, waits for them, and re-layouts  0.6 us (2%)
    pallas_call x1, Pallas kernels, shards(): pl.pallas_call(functools.partial(kernel, rows_n, cols_n), out_shape=pltpu...  29.1 us
    unnamed x1, local copies, waits for them, and re-layouts  0.6 us

profile of v7, /device:TPU:8, one launch (start us, length us, event | category | flops | bytes accessed | tf_op | source)
XLA Modules:
  0.0 29.7 jit_solution(5558194228647761936)
XLA Ops:
  0.0 29.1 %density.1 = bf16[24,256]{1,0:T(8,128)(2,1)S(1)} custom-call(bf16[4,2700]{1,0:T(4,128)(2,1)} %panels.1, s32[1,1500]{1,0:T(1,128)} %bitcast.3, bf16[1350,2700]{1,0:T(8,128)(2,1)} %amp.1, bf16[1350,1500]{1,0:T(8,128)(2,1)} %bitcast.2), custom_call_target="tpu_custom_call" | custom-call | flops 933120000 | bytes 7290000 | tf_op jit(solution)/shard_map/density/pallas_call | solution.py:277
  29.1 0.6 %copy.6 = bf16[24,256]{1,0:T(8,128)(2,1)} copy(bf16[24,256]{1,0:T(8,128)(2,1)S(1)} %density.1) | data formatting | bytes 24576

commit v8 on v7

--- a/solution.py
+++ b/solution.py
@@ -32,6 +32,7 @@
 def kernel(
     rows_n,
     cols_n,
+    aux_n,
     panels,
     owner,
     amp,
@@ -61,6 +62,9 @@
 ):
     me_r = lax.axis_index("row")
     me_c = lax.axis_index("col")
+    me_a = lax.axis_index("aux")
+    hub = aux_n - 1
+    summing = me_a == hub
     q_own, depth = panels.shape
     virt, nao = coeff_t.shape
     q_dev = rows_n * q_own
@@ -89,8 +93,18 @@
     cp_o.start()
     cp_t.start()
     cp_w.start()
-    for k in far:
-        greet(col=lax.rem(me_c + k, cols_n))
+
+    @pl.when(summing)
+    def _():
+        for k in far:
+            greet(col=lax.rem(me_c + k, cols_n))
+        for k in far + (0,):
+            greet(col=lax.rem(me_c + k, cols_n), aux=0)
+
+    @pl.when(jnp.logical_not(summing))
+    def _():
+        for k in order + (0,):
+            greet(row=row_at(k), aux=hub)
 
     x_stage[...] = jnp.zeros_like(x_stage)
     cp_p.wait()
@@ -106,7 +120,14 @@
     for t in range(chunks):
         x_all[t, own_rows, :] = x_stage[t].astype(BF16)
 
-    pl.semaphore_wait(barrier, rows_n - 1 + cols_n - 1)
+    @pl.when(summing)
+    def _():
+        pl.semaphore_wait(barrier, 2 * rows_n - 1 + cols_n - 1)
+
+    @pl.when(jnp.logical_not(summing))
+    def _():
+        pl.semaphore_wait(barrier, rows_n - 1 + cols_n)
+
 
     def panel_copy(t, source, to):
         rows = x_all.at[t, pl.ds(pl.multiple_of(source * tall, tall), tall), :]
@@ -182,13 +203,13 @@
     half = jnp.dot(split(partial), w_buf[...], preferred_element_type=F32)
     half = split(half[:q_dev] + half[q_dev:])
 
-    def partial_copy(source, to):
+    def partial_copy(aux, source, to):
         return pltpu.make_async_remote_copy(
             src_ref=d_buf.at[to],
-            dst_ref=r_buf.at[source],
+            dst_ref=r_buf.at[aux, source],
             send_sem=ds.at[0],
-            recv_sem=dr.at[0],
-            device_id={"col": to},
+            recv_sem=dr.at[aux],
+            device_id={"col": to, "aux": hub},
             device_id_type=MESH,
         )
 
@@ -216,39 +237,55 @@
         for k in (2, 1, 3, 0):
             to = quad * QUAD + lax.rem(me_c + k, QUAD)
             if step < quads - 1 or k:
-                partial_copy(me_c, to).start()
+                partial_copy(me_a, me_c, to).start()
+            else:
+
+                @pl.when(jnp.logical_not(summing))
+                def _():
+                    partial_copy(me_a, me_c, to).start()
 
     for t in range(chunks):
         sent = x_all.at[t, pl.ds(0, (rows_n - 1) * tall), :]
         pltpu.make_async_copy(sent, sent, xs.at[t]).wait()
-    others = r_buf.at[pl.ds(0, cols_n - 1)]
-    pltpu.make_async_copy(others, others, dr.at[0]).wait()
-    total = d_buf[me_c]
-    for k in range(1, cols_n):
-        total = total + r_buf[lax.rem(me_c + k, cols_n)]
-    total = jnp.concatenate([total, jnp.zeros((LANES - dense, LANES), F32)], axis=0)
-    z_buf[...] = total.T.astype(BF16)
-
-    def slot_copy(source, to):
+    def slot_copy(aux, source, to):
         return pltpu.make_async_remote_copy(
-            src_ref=z_buf.at[pl.ds(pl.multiple_of(to * HEAD, HEAD), HEAD), :],
+            src_ref=z_buf.at[aux, pl.ds(pl.multiple_of(to * HEAD, HEAD), HEAD), :],
             dst_ref=z_all.at[pl.ds(pl.multiple_of(source * HEAD, HEAD), HEAD), :],
-            send_sem=zs.at[0],
+            send_sem=zs.at[aux],
             recv_sem=zr.at[0],
-            device_id={"row": to},
+            device_id={"row": to, "aux": aux},
             device_id_type=MESH,
         )
 
-    for k in order:
-        slot_copy(me_r, row_at(k)).start()
-    own = pl.ds(pl.multiple_of(me_r * HEAD, HEAD), HEAD)
-    z_all[own, :] = z_buf[own, :]
-
-    partials_sent = d_buf.at[pl.ds(0, cols_n - 1)]
-    pltpu.make_async_copy(partials_sent, partials_sent, ds.at[0]).wait()
-
-    others = z_all.at[pl.ds(0, (rows_n - 1) * HEAD), :]
-    pltpu.make_async_copy(others, others, zr.at[0]).wait()
+    @pl.when(summing)
+    def _():
+        for aux in (hub,) + tuple(range(hub)):
+            if aux == hub:
+                others = r_buf.at[aux, pl.ds(0, cols_n - 1)]
+                total = d_buf[me_c]
+            else:
+                others = r_buf.at[aux]
+                total = jnp.zeros((dense, LANES), F32)
+            pltpu.make_async_copy(others, others, dr.at[aux]).wait()
+            for k in range(1 if aux == hub else 0, cols_n):
+                total = total + r_buf[aux, lax.rem(me_c + k, cols_n)]
+            total = jnp.concatenate([total, jnp.zeros((LANES - dense, LANES), F32)], axis=0)
+            z_buf[aux] = total.T.astype(BF16)
+            for k in order:
+                slot_copy(aux, me_r, row_at(k)).start()
+            if aux != hub:
+                slot_copy(aux, me_r, me_r).start()
+        own = pl.ds(pl.multiple_of(me_r * HEAD, HEAD), HEAD)
+        z_all[own, :] = z_buf[hub, own, :]
+        partials_sent = d_buf.at[pl.ds(0, cols_n - 1)]
+        pltpu.make_async_copy(partials_sent, partials_sent, ds.at[0]).wait()
+        others = z_all.at[pl.ds(0, (rows_n - 1) * HEAD), :]
+        pltpu.make_async_copy(others, others, zr.at[0]).wait()
+
+    @pl.when(jnp.logical_not(summing))
+    def _():
+        pltpu.make_async_copy(d_buf, d_buf, ds.at[0]).wait()
+        pltpu.make_async_copy(z_all, z_all, zr.at[0]).wait()
 
     got = jnp.concatenate([z_all[pl.ds(i * HEAD, HEAD), :] for i in range(rows_n)], axis=1)
     result = jnp.dot(got, expand[...], preferred_element_type=F32)
@@ -258,13 +295,18 @@
     )
     out[...] = jnp.concatenate([result[:, :wide], tail], axis=0).astype(BF16)
 
-    slots_sent = z_buf.at[pl.ds(0, (rows_n - 1) * HEAD), :]
-    pltpu.make_async_copy(slots_sent, slots_sent, zs.at[0]).wait()
+    @pl.when(summing)
+    def _():
+        for aux in range(aux_n):
+            parts = rows_n - 1 if aux == hub else rows_n
+            slots_sent = z_buf.at[aux, pl.ds(0, parts * HEAD), :]
+            pltpu.make_async_copy(slots_sent, slots_sent, zs.at[aux]).wait()
 
 
 def shards(panels, amplitudes, virt_coeff, row_owner):
     rows_n = lax.axis_size("row")
     cols_n = lax.axis_size("col")
+    aux_n = lax.axis_size("aux")
     q_own, depth = panels.shape
     nao, virt = virt_coeff.shape
     q_dev = rows_n * q_own
@@ -275,7 +317,7 @@
     vmem = pltpu.VMEM
     dma = pltpu.SemaphoreType.DMA
     return pl.pallas_call(
-        functools.partial(kernel, rows_n, cols_n),
+        functools.partial(kernel, rows_n, cols_n, aux_n),
         out_shape=pltpu.VMEM((HEAD + TAIL, rows_n * q_dev), BF16),
         in_specs=[pl.BlockSpec(memory_space=pl.ANY)] * 4,
         out_specs=pl.BlockSpec(memory_space=pltpu.VMEM),
@@ -291,15 +333,15 @@
             vmem((nao, cols_n // 2 * 3 * LANES), BF16),
             vmem((rows_n * LANES, 2 * rows_n * q_dev), BF16),
             vmem((cols_n, dense, LANES), F32),
-            vmem((cols_n, dense, LANES), F32),
-            vmem((rows_n * HEAD, LANES), BF16),
+            vmem((aux_n, cols_n, dense, LANES), F32),
+            vmem((aux_n, rows_n * HEAD, LANES), BF16),
             vmem((rows_n * HEAD, LANES), BF16),
             dma((4,)),
             dma((chunks,)),
             dma((chunks,)),
             dma((1,)),
-            dma((1,)),
-            dma((1,)),
+            dma((aux_n,)),
+            dma((aux_n,)),
             dma((1,)),
         ],
         compiler_params=pltpu.CompilerParams(

time: 29.8 us -> 29.7 us (level)
  no operation moved by 1% of the time
where the time goes in v8:
time: 29.7 us; the launch traced here: 29.6 us
  Pallas kernels  29 us (98%)
  local copies, waits for them, and re-layouts  0.6 us (2%)
    pallas_call x1, Pallas kernels, shards(): pl.pallas_call(functools.partial(kernel, rows_n, cols_n, aux_n), out_shap...  29 us
    unnamed x1, local copies, waits for them, and re-layouts  0.6 us

profile of v8, /device:TPU:8, one launch (start us, length us, event | category | flops | bytes accessed | tf_op | source)
XLA Modules:
  0.0 29.6 jit_solution(12833734145737499909)
XLA Ops:
  0.0 29.0 %density.1 = bf16[24,256]{1,0:T(8,128)(2,1)S(1)} custom-call(bf16[4,2700]{1,0:T(4,128)(2,1)} %panels.1, s32[1,1500]{1,0:T(1,128)} %bitcast.3, bf16[1350,2700]{1,0:T(8,128)(2,1)} %amp.1, bf16[1350,1500]{1,0:T(8,128)(2,1)} %bitcast.2), custom_call_target="tpu_custom_call" | custom-call | flops 933120000 | bytes 7290000 | tf_op jit(solution)/shard_map/density/pallas_call | solution.py:319
  29.0 0.6 %copy.6 = bf16[24,256]{1,0:T(8,128)(2,1)} copy(bf16[24,256]{1,0:T(8,128)(2,1)S(1)} %density.1) | data formatting | bytes 24576

commit v9 on v8

--- a/solution.py
+++ b/solution.py
@@ -9,7 +9,6 @@
 F32 = jnp.float32
 BF16 = jnp.bfloat16
 MESH = pl.DeviceIdType.MESH
-NT = (((1,), (1,)), ((), ()))
 
 LANES = 128
 BLOCKS = 4
@@ -39,6 +38,7 @@
     coeff_t,
     out,
     t_buf,
+    tt_buf,
     w_buf,
     p_buf,
     o_buf,
@@ -106,6 +106,35 @@
         for k in order + (0,):
             greet(row=row_at(k), aux=hub)
 
+    def fill_slots():
+        names[...] = jnp.full_like(names, -1)
+        cp_o.wait()
+        names[:, pl.ds(0, nao)] = o_buf[...]
+        tri = (iota((WIDTH, WIDTH), 0) < iota((WIDTH, WIDTH), 1)).astype(BF16)
+        carry = jnp.zeros((count, 1), F32)
+        for b in range(names.shape[1] // WIDTH):
+            name = names[:, pl.ds(b * WIDTH, WIDTH)]
+            ones = jnp.where(name == iota((count, WIDTH), 0), 1.0, 0.0).astype(F32)
+            before = jnp.dot(ones.astype(BF16), tri, preferred_element_type=F32) + carry
+            slot = jnp.sum(ones * before, axis=0, keepdims=True)
+            carry = carry + jnp.sum(ones, axis=1, keepdims=True)
+            at_row = lax.div(name, jnp.int32(cols_n))
+            at_col = name - at_row * cols_n
+            at_pair = lax.div(at_col, jnp.int32(2))
+            odd = at_col - at_pair * 2
+            base = (at_pair * pair + at_row * HEAD).astype(F32)
+            early = base + (odd * LANES).astype(F32) + slot
+            late = base + (odd * TAIL + (2 * LANES - HEAD)).astype(F32) + slot
+            lane = jnp.where(slot < HEAD, early, late)
+            lane = jnp.where(name < 0, -1.0, lane)
+            place[pl.ds(b * WIDTH, WIDTH), :] = jnp.broadcast_to(lane, (LANES, WIDTH)).T
+
+        @pl.loop(0, spread.shape[1] // LANES)
+        def _(b):
+            at = (iota((nao, LANES), 1) + b * LANES).astype(F32)
+            hot = jnp.where(place[pl.ds(0, nao), :] == at, 1.0, 0.0)
+            spread[:, pl.ds(pl.multiple_of(b * LANES, LANES), LANES)] = hot.astype(BF16)
+
     x_stage[...] = jnp.zeros_like(x_stage)
     cp_p.wait()
     for t in range(chunks):
@@ -119,6 +148,12 @@
     own_rows = pl.ds(pl.multiple_of(me_r * tall, tall), tall)
     for t in range(chunks):
         x_all[t, own_rows, :] = x_stage[t].astype(BF16)
+
+    early = me_r < rows_n // 2
+
+    @pl.when(early)
+    def _():
+        fill_slots()
 
     @pl.when(summing)
     def _():
@@ -144,33 +179,9 @@
         for k in order:
             panel_copy(t, me_r, row_at(k)).start()
 
-    names[...] = jnp.full_like(names, -1)
-    cp_o.wait()
-    names[:, pl.ds(0, nao)] = o_buf[...]
-    tri = (iota((WIDTH, WIDTH), 0) < iota((WIDTH, WIDTH), 1)).astype(BF16)
-    carry = jnp.zeros((count, 1), F32)
-    for b in range(names.shape[1] // WIDTH):
-        name = names[:, pl.ds(b * WIDTH, WIDTH)]
-        ones = jnp.where(name == iota((count, WIDTH), 0), 1.0, 0.0).astype(F32)
-        before = jnp.dot(ones.astype(BF16), tri, preferred_element_type=F32) + carry
-        slot = jnp.sum(ones * before, axis=0, keepdims=True)
-        carry = carry + jnp.sum(ones, axis=1, keepdims=True)
-        at_row = lax.div(name, jnp.int32(cols_n))
-        at_col = name - at_row * cols_n
-        at_pair = lax.div(at_col, jnp.int32(2))
-        odd = at_col - at_pair * 2
-        base = (at_pair * pair + at_row * HEAD).astype(F32)
-        early = base + (odd * LANES).astype(F32) + slot
-        late = base + (odd * TAIL + (2 * LANES - HEAD)).astype(F32) + slot
-        lane = jnp.where(slot < HEAD, early, late)
-        lane = jnp.where(name < 0, -1.0, lane)
-        place[pl.ds(b * WIDTH, WIDTH), :] = jnp.broadcast_to(lane, (LANES, WIDTH)).T
-
-    @pl.loop(0, spread.shape[1] // LANES)
-    def _(b):
-        at = (iota((nao, LANES), 1) + b * LANES).astype(F32)
-        hot = jnp.where(place[pl.ds(0, nao), :] == at, 1.0, 0.0)
-        spread[:, pl.ds(pl.multiple_of(b * LANES, LANES), LANES)] = hot.astype(BF16)
+    @pl.when(jnp.logical_not(early))
+    def _():
+        fill_slots()
 
     for i in range(rows_n):
         a = iota((LANES, rows_n * q_dev), 0)
@@ -182,6 +193,10 @@
         expand[pl.ds(i * LANES, LANES), :] = jnp.concatenate([head, tail], axis=1).astype(BF16)
 
     cp_t.wait()
+    for k in range(0, depth, WIDTH):
+        width = min(WIDTH, depth - k)
+        tt_buf[pl.ds(k, width), :] = t_buf[:, pl.ds(k, width)].T
+
     partial = jnp.zeros((q_dev, virt), F32)
     for t in range(chunks):
         others = x_all.at[t, pl.ds(0, (rows_n - 1) * tall), :]
@@ -195,8 +210,8 @@
             source = lax.div(q, q_own) * tall + kb * q_own + lax.rem(q, q_own)
             pick = jnp.where(source == iota((q_dev, LANES), 1), 1.0, 0.0).astype(BF16)
             g = jnp.dot(pick, x_all[t], preferred_element_type=F32).astype(BF16)
-            partial = partial + lax.dot_general(
-                g[:, :width], t_buf[:, pl.ds(start, width)], NT, preferred_element_type=F32
+            partial = partial + jnp.dot(
+                g[:, :width], tt_buf[pl.ds(start, width), :], preferred_element_type=F32
             )
 
     cp_w.wait()
@@ -323,6 +338,7 @@
         out_specs=pl.BlockSpec(memory_space=pltpu.VMEM),
         scratch_shapes=[
             vmem(amplitudes.shape, BF16),
+            vmem((depth, virt), BF16),
             vmem((virt, nao), BF16),
             vmem(panels.shape, BF16),
             vmem((1, nao), jnp.int32),

time: 29.7 us -> 30.4 us (1.024)
  the two profiles are of different devices: /device:TPU:8 before, /device:TPU:1 now
where the time goes in v9:
time: 30.4 us; the launch traced here: 30.3 us
  Pallas kernels  29.7 us (98%)
  local copies, waits for them, and re-layouts  0.6 us (2%)
    pallas_call x1, Pallas kernels, shards(): pl.pallas_call(functools.partial(kernel, rows_n, cols_n, aux_n), out_shap...  29.7 us

profile of v9, /device:TPU:1, one launch (start us, length us, event | category | flops | bytes accessed | tf_op | source)
XLA Modules:
  0.0 30.3 jit_solution(7442018308720240601)
XLA Ops:
  0.0 29.7 %density.1 = bf16[24,256]{1,0:T(8,128)(2,1)S(1)} custom-call(bf16[4,2700]{1,0:T(4,128)(2,1)} %panels.1, s32[1,1500]{1,0:T(1,128)} %bitcast.3, bf16[1350,2700]{1,0:T(8,128)(2,1)} %amp.1, bf16[1350,1500]{1,0:T(8,128)(2,1)} %bitcast.2), custom_call_target="tpu_custom_call" | custom-call | flops 933120000 | bytes 7290000 | tf_op jit(solution)/shard_map/density/pallas_call | solution.py:334
  29.7 0.6 %copy.6 = bf16[24,256]{1,0:T(8,128)(2,1)} copy(bf16[24,256]{1,0:T(8,128)(2,1)S(1)} %density.1) | data formatting | bytes 24576

commit v10 on v8

--- a/solution.py
+++ b/solution.py
@@ -129,20 +129,24 @@
         pl.semaphore_wait(barrier, rows_n - 1 + cols_n)
 
 
-    def panel_copy(t, source, to):
-        rows = x_all.at[t, pl.ds(pl.multiple_of(source * tall, tall), tall), :]
+    groups = ((0, 1), (1, chunks - 1))
+
+    def panel_copy(g, source, to):
+        rows = x_all.at[
+            pl.ds(*groups[g]), pl.ds(pl.multiple_of(source * tall, tall), tall), :
+        ]
         return pltpu.make_async_remote_copy(
             src_ref=rows,
             dst_ref=rows,
-            send_sem=xs.at[t],
-            recv_sem=xr.at[t],
+            send_sem=xs.at[g],
+            recv_sem=xr.at[g],
             device_id={"row": to},
             device_id_type=MESH,
         )
 
-    for t in range(chunks):
+    for g in range(len(groups)):
         for k in order:
-            panel_copy(t, me_r, row_at(k)).start()
+            panel_copy(g, me_r, row_at(k)).start()
 
     names[...] = jnp.full_like(names, -1)
     cp_o.wait()
@@ -184,8 +188,10 @@
     cp_t.wait()
     partial = jnp.zeros((q_dev, virt), F32)
     for t in range(chunks):
-        others = x_all.at[t, pl.ds(0, (rows_n - 1) * tall), :]
-        pltpu.make_async_copy(others, others, xr.at[t]).wait()
+        for g, (first, size) in enumerate(groups):
+            if t == first:
+                others = x_all.at[pl.ds(first, size), pl.ds(0, (rows_n - 1) * tall), :]
+                pltpu.make_async_copy(others, others, xr.at[g]).wait()
         for kb in range(BLOCKS):
             start = (t * BLOCKS + kb) * WIDTH
             width = min(WIDTH, depth - start)
@@ -194,9 +200,9 @@
             q = iota((q_dev, LANES), 0)
             source = lax.div(q, q_own) * tall + kb * q_own + lax.rem(q, q_own)
             pick = jnp.where(source == iota((q_dev, LANES), 1), 1.0, 0.0).astype(BF16)
-            g = jnp.dot(pick, x_all[t], preferred_element_type=F32).astype(BF16)
+            part = jnp.dot(pick, x_all[t], preferred_element_type=F32).astype(BF16)
             partial = partial + lax.dot_general(
-                g[:, :width], t_buf[:, pl.ds(start, width)], NT, preferred_element_type=F32
+                part[:, :width], t_buf[:, pl.ds(start, width)], NT, preferred_element_type=F32
             )
 
     cp_w.wait()
@@ -244,9 +250,9 @@
                 def _():
                     partial_copy(me_a, me_c, to).start()
 
-    for t in range(chunks):
-        sent = x_all.at[t, pl.ds(0, (rows_n - 1) * tall), :]
-        pltpu.make_async_copy(sent, sent, xs.at[t]).wait()
+    for g in range(len(groups)):
+        sent = x_all.at[pl.ds(*groups[g]), pl.ds(0, (rows_n - 1) * tall), :]
+        pltpu.make_async_copy(sent, sent, xs.at[g]).wait()
     def slot_copy(aux, source, to):
         return pltpu.make_async_remote_copy(
             src_ref=z_buf.at[aux, pl.ds(pl.multiple_of(to * HEAD, HEAD), HEAD), :],

time: 29.7 us -> 30.1 us (1.013)
  Pallas kernels: 29 us -> 29.4 us
    pallas_call x1, Pallas kernels: 29 us -> 29.4 us  [shards(): pl.pallas_call(functools.partial(kernel, rows_n, cols_n, aux_n), out_shap...]
where the time goes in v10:
time: 30.1 us; the launch traced here: 30 us
  Pallas kernels  29.4 us (98%)
  local copies, waits for them, and re-layouts  0.6 us (2%)
    pallas_call x1, Pallas kernels, shards(): pl.pallas_call(functools.partial(kernel, rows_n, cols_n, aux_n), out_shap...  29.4 us
    unnamed x1, local copies, waits for them, and re-layouts  0.6 us

profile of v10, /device:TPU:8, one launch (start us, length us, event | category | flops | bytes accessed | tf_op | source)
XLA Modules:
  0.0 30.0 jit_solution(14577359076634540951)
XLA Ops:
  0.0 29.4 %density.1 = bf16[24,256]{1,0:T(8,128)(2,1)S(1)} custom-call(bf16[4,2700]{1,0:T(4,128)(2,1)} %panels.1, s32[1,1500]{1,0:T(1,128)} %bitcast.3, bf16[1350,2700]{1,0:T(8,128)(2,1)} %amp.1, bf16[1350,1500]{1,0:T(8,128)(2,1)} %bitcast.2), custom_call_target="tpu_custom_call" | custom-call | flops 933120000 | bytes 7290000 | tf_op jit(solution)/shard_map/density/pallas_call | solution.py:325
  29.4 0.6 %copy.6 = bf16[24,256]{1,0:T(8,128)(2,1)} copy(bf16[24,256]{1,0:T(8,128)(2,1)S(1)} %density.1) | data formatting | bytes 24576

commit v11 on v9

--- a/solution.py
+++ b/solution.py
@@ -9,6 +9,7 @@
 F32 = jnp.float32
 BF16 = jnp.bfloat16
 MESH = pl.DeviceIdType.MESH
+NT = (((1,), (1,)), ((), ()))
 
 LANES = 128
 BLOCKS = 4
@@ -38,7 +39,6 @@
     coeff_t,
     out,
     t_buf,
-    tt_buf,
     w_buf,
     p_buf,
     o_buf,
@@ -193,10 +193,6 @@
         expand[pl.ds(i * LANES, LANES), :] = jnp.concatenate([head, tail], axis=1).astype(BF16)
 
     cp_t.wait()
-    for k in range(0, depth, WIDTH):
-        width = min(WIDTH, depth - k)
-        tt_buf[pl.ds(k, width), :] = t_buf[:, pl.ds(k, width)].T
-
     partial = jnp.zeros((q_dev, virt), F32)
     for t in range(chunks):
         others = x_all.at[t, pl.ds(0, (rows_n - 1) * tall), :]
@@ -210,8 +206,8 @@
             source = lax.div(q, q_own) * tall + kb * q_own + lax.rem(q, q_own)
             pick = jnp.where(source == iota((q_dev, LANES), 1), 1.0, 0.0).astype(BF16)
             g = jnp.dot(pick, x_all[t], preferred_element_type=F32).astype(BF16)
-            partial = partial + jnp.dot(
-                g[:, :width], tt_buf[pl.ds(start, width), :], preferred_element_type=F32
+            partial = partial + lax.dot_general(
+                g[:, :width], t_buf[:, pl.ds(start, width)], NT, preferred_element_type=F32
             )
 
     cp_w.wait()
@@ -338,7 +334,6 @@
         out_specs=pl.BlockSpec(memory_space=pltpu.VMEM),
         scratch_shapes=[
             vmem(amplitudes.shape, BF16),
-            vmem((depth, virt), BF16),
             vmem((virt, nao), BF16),
             vmem(panels.shape, BF16),
             vmem((1, nao), jnp.int32),

time: 30.4 us -> 29.7 us (0.977)
  the two profiles are of different devices: /device:TPU:1 before, /device:TPU:8 now
where the time goes in v11:
time: 29.7 us; the launch traced here: 29.6 us
  Pallas kernels  29 us (98%)
  local copies, waits for them, and re-layouts  0.6 us (2%)
    pallas_call x1, Pallas kernels, shards(): pl.pallas_call(functools.partial(kernel, rows_n, cols_n, aux_n), out_shap...  29 us
    unnamed x1, local copies, waits for them, and re-layouts  0.6 us

profile of v11, /device:TPU:8, one launch (start us, length us, event | category | flops | bytes accessed | tf_op | source)
XLA Modules:
  0.0 29.6 jit_solution(18311587651571245042)
XLA Ops:
  0.0 29.0 %density.1 = bf16[24,256]{1,0:T(8,128)(2,1)S(1)} custom-call(bf16[4,2700]{1,0:T(4,128)(2,1)} %panels.1, s32[1,1500]{1,0:T(1,128)} %bitcast.3, bf16[1350,2700]{1,0:T(8,128)(2,1)} %amp.1, bf16[1350,1500]{1,0:T(8,128)(2,1)} %bitcast.2), custom_call_target="tpu_custom_call" | custom-call | flops 933120000 | bytes 7290000 | tf_op jit(solution)/shard_map/density/pallas_call | solution.py:330
  29.0 0.6 %copy.6 = bf16[24,256]{1,0:T(8,128)(2,1)} copy(bf16[24,256]{1,0:T(8,128)(2,1)S(1)} %density.1) | data formatting | bytes 24576

commit v12 on v8

--- a/solution.py
+++ b/solution.py
@@ -85,6 +85,18 @@
 
     for k in order:
         greet(row=row_at(k))
+    @pl.when(summing)
+    def _():
+        for k in far + (0,):
+            greet(col=lax.rem(me_c + k, cols_n), aux=0)
+        for k in far:
+            greet(col=lax.rem(me_c + k, cols_n))
+
+    @pl.when(jnp.logical_not(summing))
+    def _():
+        for k in order + (0,):
+            greet(row=row_at(k), aux=hub)
+
     cp_p = pltpu.make_async_copy(panels, p_buf, local_sem.at[0])
     cp_o = pltpu.make_async_copy(owner, o_buf, local_sem.at[1])
     cp_t = pltpu.make_async_copy(amp, t_buf, local_sem.at[2])
@@ -93,18 +105,6 @@
     cp_o.start()
     cp_t.start()
     cp_w.start()
-
-    @pl.when(summing)
-    def _():
-        for k in far:
-            greet(col=lax.rem(me_c + k, cols_n))
-        for k in far + (0,):
-            greet(col=lax.rem(me_c + k, cols_n), aux=0)
-
-    @pl.when(jnp.logical_not(summing))
-    def _():
-        for k in order + (0,):
-            greet(row=row_at(k), aux=hub)
 
     x_stage[...] = jnp.zeros_like(x_stage)
     cp_p.wait()

time: 29.7 us -> 29.7 us (level)
  no operation moved by 1% of the time
where the time goes in v12:
time: 29.7 us; the launch traced here: 29.6 us
  Pallas kernels  29 us (98%)
  local copies, waits for them, and re-layouts  0.6 us (2%)
    pallas_call x1, Pallas kernels, shards(): pl.pallas_call(functools.partial(kernel, rows_n, cols_n, aux_n), out_shap...  29 us
    unnamed x1, local copies, waits for them, and re-layouts  0.6 us

profile of v12, /device:TPU:8, one launch (start us, length us, event | category | flops | bytes accessed | tf_op | source)
XLA Modules:
  0.0 29.6 jit_solution(2646979782240409137)
XLA Ops:
  0.0 29.0 %density.1 = bf16[24,256]{1,0:T(8,128)(2,1)S(1)} custom-call(bf16[4,2700]{1,0:T(4,128)(2,1)} %panels.1, s32[1,1500]{1,0:T(1,128)} %bitcast.3, bf16[1350,2700]{1,0:T(8,128)(2,1)} %amp.1, bf16[1350,1500]{1,0:T(8,128)(2,1)} %bitcast.2), custom_call_target="tpu_custom_call" | custom-call | flops 933120000 | bytes 7290000 | tf_op jit(solution)/shard_map/density/pallas_call | solution.py:319
  29.0 0.6 %copy.6 = bf16[24,256]{1,0:T(8,128)(2,1)} copy(bf16[24,256]{1,0:T(8,128)(2,1)S(1)} %density.1) | data formatting | bytes 24576

commit v13 on v11

--- a/solution.py
+++ b/solution.py
@@ -85,6 +85,18 @@
 
     for k in order:
         greet(row=row_at(k))
+    @pl.when(summing)
+    def _():
+        for k in far + (0,):
+            greet(col=lax.rem(me_c + k, cols_n), aux=0)
+        for k in far:
+            greet(col=lax.rem(me_c + k, cols_n))
+
+    @pl.when(jnp.logical_not(summing))
+    def _():
+        for k in order + (0,):
+            greet(row=row_at(k), aux=hub)
+
     cp_p = pltpu.make_async_copy(panels, p_buf, local_sem.at[0])
     cp_o = pltpu.make_async_copy(owner, o_buf, local_sem.at[1])
     cp_t = pltpu.make_async_copy(amp, t_buf, local_sem.at[2])
@@ -93,18 +105,6 @@
     cp_o.start()
     cp_t.start()
     cp_w.start()
-
-    @pl.when(summing)
-    def _():
-        for k in far:
-            greet(col=lax.rem(me_c + k, cols_n))
-        for k in far + (0,):
-            greet(col=lax.rem(me_c + k, cols_n), aux=0)
-
-    @pl.when(jnp.logical_not(summing))
-    def _():
-        for k in order + (0,):
-            greet(row=row_at(k), aux=hub)
 
     def fill_slots():
         names[...] = jnp.full_like(names, -1)

time: 29.7 us -> 29.6 us (level)
  no operation moved by 1% of the time
where the time goes in v13:
time: 29.6 us
  Pallas kernels  29 us (98%)
  local copies, waits for them, and re-layouts  0.6 us (2%)
    pallas_call x1, Pallas kernels, shards(): pl.pallas_call(functools.partial(kernel, rows_n, cols_n, aux_n), out_shap...  29 us
    unnamed x1, local copies, waits for them, and re-layouts  0.6 us

profile of v13, /device:TPU:8, one launch (start us, length us, event | category | flops | bytes accessed | tf_op | source)
XLA Modules:
  0.0 29.6 jit_solution(9408001859664346886)
XLA Ops:
  0.0 29.0 %density.1 = bf16[24,256]{1,0:T(8,128)(2,1)S(1)} custom-call(bf16[4,2700]{1,0:T(4,128)(2,1)} %panels.1, s32[1,1500]{1,0:T(1,128)} %bitcast.3, bf16[1350,2700]{1,0:T(8,128)(2,1)} %amp.1, bf16[1350,1500]{1,0:T(8,128)(2,1)} %bitcast.2), custom_call_target="tpu_custom_call" | custom-call | flops 933120000 | bytes 7290000 | tf_op jit(solution)/shard_map/density/pallas_call | solution.py:330
  29.0 0.6 %copy.6 = bf16[24,256]{1,0:T(8,128)(2,1)} copy(bf16[24,256]{1,0:T(8,128)(2,1)S(1)} %density.1) | data formatting | bytes 24576
